TPU v7x, 32 devices: a whole 2x2x4 slice. The times are simulated.
32 devices in a mesh: wide: 8 (over y, x, core), narrow: 4 (over z).
Axes of the slice: x: 2, y: 2, z: 4, core: 2. Of those that a mesh axis runs over, the one named last changes fastest.
Arguments:
- amplitudes: bfloat16 [48, 2, 1536, 1536], P('narrow', None, 'wide'), may hold values from -6 to 6
- pair_integrals: bfloat16 [48, 2, 1536, 1536], P('narrow', None, 'wide'), may hold values from -4 to 4
- cycle_integrals: bfloat16 [2, 1536, 2, 1536], P(None, None, None, 'narrow'), may hold values from -0.109375 to 0.109375
- ladder_integrals: bfloat16 [4, 4, 1536, 1536], P(None, None, 'wide', 'narrow'), may hold values from -0.078125 to 0.078125
- occ_energy: float32 [300], replicated, may hold values from -2 to -0.5
- virt_energy: float32 [1536], replicated, may hold values from 0.3 to 3
- occ_irrep: int32 [300], replicated, may hold values from 0 to 1
- virt_irrep: int32 [96], replicated, may hold values from 0 to 1
- slab_i: int32 [48], P('narrow'), may hold values from 0 to 299
- slab_j: int32 [2], replicated, may hold values from 0 to 299
Outputs:
- new_amplitudes: bfloat16 [48, 2, 1536, 1536], P('narrow', None, 'wide')
Inputs may be any that keep to these rules, and one draw needn't show every extreme that they name: `slab_i`: each entry names an occupied orbital. `slab_j`: each entry names an occupied orbital.
All inputs are finite; a program needn't handle non-finite values.
Results may differ from a plain program's by a relative error of at most 0.0046.
Values may be sent and summed in bfloat16 or wider, within the bound.
No kernel may reach another device: no remote copies, remote signals or barrier semaphores. Data moves between devices by JAX's collectives and lax.ppermute only.
A program may use at most 192 MiB of HBM per device.

v0:
```python
import jax
import jax.numpy as jnp
from jax import lax
from jax.sharding import PartitionSpec as P

VBLK = 16


def spread(value, axis, source):
    kept = jnp.where(lax.axis_index(axis) == source, value, 0).astype(value.dtype)
    return lax.psum(kept, axis)


def lookup(indices, values_table):
    table_size = values_table.shape[0]
    matches = indices[:, None] == jnp.arange(table_size, dtype=jnp.int32)[None, :]
    return jnp.sum(
        jnp.where(matches, values_table[None, :], jnp.zeros_like(values_table)[None, :]), axis=1
    )


def cycle_product(amp_rows, weights):
    inner_k, inner_c, outer_j, outer_a = weights.shape
    flat_weights = weights.reshape(inner_k * inner_c, outer_j * outer_a)

    def one_row(amp_row):
        flat_row = amp_row.reshape(inner_k * inner_c, amp_row.shape[2])
        product = lax.dot_general(
            flat_weights, flat_row, (((0,), (0,)), ((), ())), preferred_element_type=jnp.float32
        )
        return product.reshape(outer_j, outer_a, amp_row.shape[2]).astype(jnp.bfloat16)

    return lax.map(one_row, amp_rows)


def per_device(
    amplitudes,
    pair_integrals,
    cycle_integrals,
    ladder_integrals,
    occ_energy,
    virt_energy,
    occ_irrep,
    virt_irrep,
    slab_i,
    slab_j,
):
    wide_count = lax.axis_size("wide")
    wide_index = lax.axis_index("wide")
    tile_width = ladder_integrals.shape[0]
    virt_count = virt_energy.shape[0]
    row_count = virt_count // wide_count
    relaid = lax.all_to_all(amplitudes, "wide", split_axis=3, concat_axis=2, tiled=True)
    tile_amps = spread(amplitudes[:, :, :tile_width, :], "wide", 0)
    ladder = jnp.einsum(
        "ijcd,acbd->ijab",
        tile_amps,
        lax.all_gather(ladder_integrals, "narrow", axis=3, tiled=True),
        preferred_element_type=jnp.float32,
    )
    cycle_local = cycle_product(
        relaid, lax.all_gather(cycle_integrals, "narrow", axis=3, tiled=True)
    )
    coupled_local = (
        cycle_local.astype(jnp.float32).at[:, :, :tile_width, :].add(ladder).astype(jnp.bfloat16)
    )
    coupled = lax.all_to_all(coupled_local, "wide", split_axis=2, concat_axis=3, tiled=True)
    energy_first = lookup(slab_i, occ_energy)
    energy_second = lookup(slab_j, occ_energy)
    label_first = lookup(slab_i, occ_irrep)
    label_second = lookup(slab_j, occ_irrep)
    label_virt = jnp.repeat(virt_irrep, VBLK)
    energy_rows = lax.dynamic_slice_in_dim(virt_energy, wide_index * row_count, row_count)
    label_rows = lax.dynamic_slice_in_dim(label_virt, wide_index * row_count, row_count)
    residual = pair_integrals.astype(jnp.float32) + coupled.astype(jnp.float32)
    denominator = (
        energy_rows[None, None, :, None]
        + virt_energy[None, None, None, :]
        - energy_first[:, None, None, None]
        - energy_second[None, :, None, None]
    )
    parity = (
        label_first[:, None, None, None]
        + label_second[None, :, None, None]
        + label_rows[None, None, :, None]
        + label_virt[None, None, None, :]
    ) % 2
    allowed = (1 - parity).astype(jnp.float32)
    return (allowed * residual / denominator).astype(jnp.bfloat16)


def solution(mesh):
    return jax.shard_map(
        per_device,
        mesh=mesh,
        in_specs=(
            P("narrow", None, "wide", None),
            P("narrow", None, "wide", None),
            P(None, None, None, "narrow"),
            P(None, None, "wide", "narrow"),
            P(),
            P(),
            P(),
            P(),
            P("narrow"),
            P(),
        ),
        out_specs=P("narrow", None, "wide", None),
        check_vma=False,
    )
```

profile of v0, /device:TPU:0, one launch (start us, length us, event | category | flops | bytes accessed | tf_op | source)
XLA Modules:
  0.0 1099.7 jit_solution(12022871699554408921)
XLA Ops:
  10.6 31.1 %copy.37 = bf16[12,2,192,1536]{2,0,1,3:T(8,128)(2,1)} copy(bf16[12,2,192,1536]{3,2,1,0:T(8,128)(2,1)} %param.14) | data formatting | bytes 28311552 | tf_op args[0]
  48.1 276.1 %all-to-all-done = bf16[12,2,192,1536]{2,0,1,3:T(8,128)(2,1)} async-done(((bf16[12,2,192,1536]{2,0,1,3:T(8,128)(2,1)}), bf16[12,2,192,1536]{2,0,1,3:T(8,128)(2,1)}, u32[]{:S(2)}, u32[]{:S(2)}) %all-to-all-start) | async-done | bytes 14155808 | tf_op jit(solution)/shard_map/all_to_all | solution.py:53
  324.2 33.4 %copy.38 = bf16[12,2,8,192,192]{4,3,2,1,0:T(8,128)(2,1)} copy(bf16[12,2,8,192,192]{3,0,1,4,2:T(8,128)(2,1)} %bitcast.3) | data formatting | bytes 28311552 | tf_op jit(solution)/shard_map/all_to_all | solution.py:53
  366.6 136.4 %all-gather.3.cloned.1.call-done = bf16[2,1536,2,1536]{3,2,1,0:T(2,128)(2,1)} async-done(((bf16[2,1536,2,384]{3,2,1,0:T(2,128)(2,1)}), bf16[2,1536,2,1536]{3,2,1,0:T(2,128)(2,1)}) %all-gather.3.cloned.1.call-update) | async-done | bytes 18874384 | tf_op jit(solution)/shard_map/all_gather | solution.py:62
  503.0 19.7 %copy.49 = bf16[384,8,2,1536]{3,1,2,0:T(8,128)(2,1)} copy(bf16[384,8,2,1536]{3,2,1,0:T(2,128)(2,1)} %bitcast.44) | data formatting | bytes 37748736
  522.7 145.7 %while.11 = (s32[]{:T(128)}, bf16[12,2,1536,192]{2,3,1,0:T(8,128)(2,1)}, bf16[12,2,1536,192]{3,2,1,0:T(8,128)(2,1)}, bf16[3072,3072]{1,0:T(8,128)(2,1)}, s32[]{:T(128)}) while((s32[]{:T(128)}, bf16[12,2,1536,192]{2,3,1,0:T(8,128)(2,1)}, bf16[12,2,1536,192]{3,2,1,0:T(8,128)(2,1)}, bf16[3072,3072]{1,0:T(8,128)(2,1)}, s32[]{:T(128)}) %tuple.32), condition=%wide.region_3.4_spmd, body=%wide.region_2.3_spmd.sunk | while | flops 3624468480 | bytes 28311628 | solution.py:33
  524.3 8.6 fusion.20
  536.4 8.6 fusion.20
  548.5 8.6 fusion.20
  560.7 8.6 fusion.20
  572.8 8.6 fusion.20
  585.0 8.6 fusion.20
  597.1 8.6 fusion.20
  609.3 8.6 fusion.20
  621.4 8.6 fusion.20
  676.6 9.3 copy-done
  686.4 9.0 scatter-add.4
  695.4 15.3 %convert_element_type.48 = bf16[12,2,1536,192]{2,3,1,0:T(8,128)(2,1)} convert(f32[12,2,1536,192]{2,3,1,0:T(8,128)} %scatter-add.4) | non-fusion elementwise | flops 7077888 | bytes 42467328 | tf_op jit(solution)/shard_map/convert_element_type | solution.py:65
  710.7 46.4 %copy.42 = bf16[12,2,1536,192]{3,1,0,2:T(2,128)(2,1)} copy(bf16[12,2,1536,192]{2,3,1,0:T(8,128)(2,1)} %convert_element_type.48) | data formatting | bytes 28311552 | tf_op jit(solution)/shard_map/convert_element_type | solution.py:65
  771.6 197.9 %all-to-all-done.1 = bf16[12,2,1536,192]{3,1,0,2:T(2,128)(2,1)} async-done(((bf16[12,2,1536,192]{3,1,0,2:T(2,128)(2,1)}), bf16[12,2,1536,192]{3,1,0,2:T(2,128)(2,1)}, u32[]{:S(2)}, u32[]{:S(2)}) %all-to-all-start.1) | async-done | bytes 14155808 | tf_op jit(solution)/shard_map/all_to_all | solution.py:67
  969.6 20.2 %convert_bitcast_fusion = f32[12,2,192,8,192]{4,1,0,2,3:T(2,128)} fusion(bf16[12,2,8,192,192]{4,1,0,3,2:T(2,128)(2,1)} %bitcast.14), kind=kLoop, calls=%fused_computation.9 | loop fusion | flops 7077888 | bytes 42467328 | tf_op jit(solution)/shard_map/convert_element_type | solution.py:75
  989.7 35.6 %copy.43 = f32[12,2,192,8,192]{4,3,2,1,0:T(8,128)} copy(f32[12,2,192,8,192]{4,1,0,2,3:T(2,128)} %convert_bitcast_fusion) | data formatting | bytes 56623104 | tf_op jit(solution)/shard_map/convert_element_type | solution.py:75
  1025.3 37.5 %reshape.149 = f32[12,2,192,1536]{3,2,1,0:T(8,128)} reshape(f32[12,2,192,8,192]{4,3,2,1,0:T(8,128)} %copy.43) | data formatting | bytes 56623104 | tf_op jit(solution)/shard_map/convert_element_type | solution.py:75
  1062.8 29.5 %fusion.6 = bf16[12,2,192,1536]{3,2,1,0:T(8,128)(2,1)} fusion(f32[12,2,192,1536]{3,2,1,0:T(8,128)} %reshape.149, bf16[12,2,192,1536]{3,2,1,0:T(8,128)(2,1)} %param.15, f32[2]{0:T(128)S(1)} %select_reduce_fusion.2, f32[12,192,1536]{2,1,0:T(8,128)} %broadcast_subtract_fusion, s32[1536]{0:T(1024)S(1)} %reshape.147, s32[12,2,192]{2,1,0:T(2,128)S(1)} %broadcast_add_fusion.1), kind=kLoop, calls=%fused_computation.15 | loop fusion | flops 141557760 | bytes 70803464 | tf_op jit(solution)/shard_map/convert_element_type | solution.py:89
  (83 shorter events, 109.9 us)
Async XLA Ops:
  7.4 350.3 %all-reduce.2.cloned.1.call-start = ((), (), s32[]{:S(2)}) async-start(), calls=%async_computation.3 | async-start | bytes 786432 | tf_op jit(solution)/shard_map/psum | solution.py:11
  9.4 348.2 %all-gather.5.cloned.1.call-start = ((), (), s32[]{:S(2)}) async-start(), calls=%async_computation.4 | async-start | bytes 11796480 | tf_op jit(solution)/shard_map/all_gather | solution.py:58
  10.0 493.0 %all-gather.3.cloned.1.call-start = ((), (), s32[]{:S(2)}) async-start(), calls=%async_computation.2 | async-start | bytes 23592960 | tf_op jit(solution)/shard_map/all_gather | solution.py:62
  41.6 282.6 %all-to-all-start = ((bf16[12,2,192,1536]{2,0,1,3:T(8,128)(2,1)}), bf16[12,2,192,1536]{2,0,1,3:T(8,128)(2,1)}, u32[]{:S(2)}, u32[]{:S(2)}) async-start(bf16[12,2,192,1536]{2,0,1,3:T(8,128)(2,1)} %copy.37), calls=%async_computation | async-start | bytes 50331648 | tf_op jit(solution)/shard_map/all_to_all | solution.py:53
  668.5 17.5 %copy-start.1 = (f32[12,2,4,192]{2,3,1,0:T(8,128)S(1)}, f32[12,2,4,192]{2,3,1,0:T(8,128)}, u32[]{:S(2)}) copy-start(f32[12,2,4,192]{2,3,1,0:T(8,128)} %copy.41) | copy-start | bytes 221188
  676.6 9.4 copy-start
  757.1 6.3 copy-start.7
  757.1 6.4 copy-start.2
  757.1 6.6 copy-start.3
  757.1 6.6 copy-start.5
  757.1 6.8 copy-start.6
  757.1 6.9 copy-start.4
  757.1 212.5 %all-to-all-start.1 = ((bf16[12,2,1536,192]{3,1,0,2:T(2,128)(2,1)}), bf16[12,2,1536,192]{3,1,0,2:T(2,128)(2,1)}, u32[]{:S(2)}, u32[]{:S(2)}) async-start(bf16[12,2,1536,192]{3,1,0,2:T(2,128)(2,1)} %copy.42), calls=%async_computation.1 | async-start | bytes 37748736 | tf_op jit(solution)/shard_map/all_to_all | solution.py:67
Sparse Core Ops, SparseCore 0:
  11.3 113.6 all-reduce.1
Sparse Core Ops, SparseCore 1:
  11.5 169.3 all-gather.4
  182.2 320.7 all-gather.2
where the time goes:
time: 1110 us; the launch traced here: 1100 us
  waiting for transfers between devices  612 us (55%)
  local copies, waits for them, and re-layouts  268 us (24%)
  matrix products  110 us (10%)
  other arithmetic  82.3 us (7%)
  between operations  15 us (1%)
  starting transfers between devices  12.7 us (1%)
    all_to_all x1, waiting for transfers between devices, per_device(): lax.all_to_all(amplitudes, 'wide', split_axis=3, concat_axis=2, tiled=True)  276 us
    all_to_all x1, waiting for transfers between devices, per_device(): lax.all_to_all(coupled_local, 'wide', split_axis=2, concat_axis=3, tiled=...  198 us
    all_gather x1, waiting for transfers between devices, per_device(): lax.all_gather(cycle_integrals, 'narrow', axis=3, tiled=True)  136 us
    dot_general x12, matrix products, one_row(): lax.dot_general(flat_weights, flat_row, (((0,), (0,)), ((), ())), preferr...  103 us
    convert_element_type x2, local copies, waits for them, and re-layouts, per_device(): residual = pair_integrals.astype(jnp.float32) + coupled.astype(jnp.float32)  73.1 us
    unnamed x18, local copies, waits for them, and re-layouts  60.2 us
    convert_element_type x1, local copies, waits for them, and re-layouts, per_device(): cycle_local.astype(jnp.float32).at[:, :, :tile_width, :].add(ladder)  46.4 us
    all_to_all x1, local copies, waits for them, and re-layouts, per_device(): lax.all_to_all(amplitudes, 'wide', split_axis=3, concat_axis=2, tiled=True)  33.4 us
  transfers between devices with their start and end apart: 5, of which 3 were waited for; matrix products, arithmetic and copies ran while one was open for 7% of the time, Pallas kernels for 0%

commit v1 on v0

--- a/solution.py
+++ b/solution.py
@@ -1,9 +1,16 @@
+import functools
+
 import jax
 import jax.numpy as jnp
 from jax import lax
+from jax.experimental import pallas as pl
+from jax.experimental.pallas import tpu as pltpu
 from jax.sharding import PartitionSpec as P
 
 VBLK = 16
+CORE, XBIT, YBIT = 1, 2, 4
+LANES = 512
+VMEM = 60 * 2**20
 
 
 def spread(value, axis, source):
@@ -33,7 +40,7 @@
     return lax.map(one_row, amp_rows)
 
 
-def per_device(
+def per_device_any(
     amplitudes,
     pair_integrals,
     cycle_integrals,
@@ -89,7 +96,348 @@
     return (allowed * residual / denominator).astype(jnp.bfloat16)
 
 
+def launch_kernel(extended, passed, *refs):
+    outs = refs[len(refs) - len(extended) - passed :]
+    for out, extra in zip(outs, extended):
+        rows = refs[0].shape[2]
+        out[0, 0, pl.ds(0, rows), :] = refs[0][0, 0]
+        if extra:
+            out[0, 0, pl.ds(rows, out.shape[2] - rows), :] = refs[1][0, 0]
+        refs = refs[1 + extra :]
+
+
+def launch(cuts, handed_on, waited_for):
+    anywhere = pl.BlockSpec(memory_space=pl.ANY)
+    operands, in_specs, out_specs, out_shape = [], [], [], []
+    second = 1
+    for array, index, extra in cuts:
+        _, second, rows, cols = array.shape
+        operands.append(array)
+        in_specs.append(pl.BlockSpec((1, 1, rows, cols), lambda j, index=index: (index, j, 0, 0)))
+        if extra is not None:
+            operands.append(extra)
+            in_specs.append(pl.BlockSpec((1, 1, *extra.shape[2:]), lambda j: (0, j, 0, 0)))
+            rows += extra.shape[2]
+        out_specs.append(pl.BlockSpec((1, 1, rows, cols), lambda j: (0, j, 0, 0)))
+        out_shape.append(jax.ShapeDtypeStruct((1, second, rows, cols), array.dtype))
+    aliases = {len(operands) + n: len(cuts) + n for n in range(len(handed_on))}
+    in_specs += [anywhere for _ in [*handed_on, *waited_for]]
+    out_specs += [anywhere for _ in handed_on]
+    out_shape += [jax.ShapeDtypeStruct(value.shape, value.dtype) for value in handed_on]
+    outs = pl.pallas_call(
+        functools.partial(launch_kernel, tuple(extra is not None for *_, extra in cuts), len(handed_on)),
+        grid=(second,),
+        out_shape=tuple(out_shape),
+        in_specs=in_specs,
+        out_specs=tuple(out_specs),
+        input_output_aliases=aliases,
+        compiler_params=pltpu.CompilerParams(vmem_limit_bytes=VMEM),
+        cost_estimate=pl.CostEstimate(flops=0, bytes_accessed=1, transcendentals=0),
+        name="launch",
+    )(*operands, *handed_on, *waited_for)
+    return list(outs[: len(cuts)]), list(outs[len(cuts) :])
+
+
+def blocks_kernel(place, weights, after, out_ref, turned):
+    inner_k, row_count, outer_j, _ = weights.shape
+    depth = inner_k * row_count
+    flat = weights[...].reshape(depth * outer_j, weights.shape[3])
+    row = lax.broadcasted_iota(jnp.int32, (depth * outer_j, depth), 0)
+    col = lax.broadcasted_iota(jnp.int32, (depth * outer_j, depth), 1)
+    mine = pl.ds(pl.multiple_of(place[1] * row_count, row_count), row_count)
+    for j in range(outer_j):
+        picked = (row == outer_j * col + j).astype(weights.dtype)
+        turned[...] = lax.dot_general(flat, picked, (((0,), (0,)), ((), ())), preferred_element_type=jnp.float32)
+        out_ref[0, pl.ds(j * row_count, row_count), :] = turned[mine, :].astype(out_ref.dtype)
+
+
+def weight_blocks(first, core, count, cycle_integrals, row_count, after):
+    inner_k, _, outer_j, width = cycle_integrals.shape
+    shape = (outer_j * row_count, inner_k * row_count)
+    return pl.pallas_call(
+        blocks_kernel,
+        out_shape=jax.ShapeDtypeStruct((count, *shape), cycle_integrals.dtype),
+        grid_spec=pltpu.PrefetchScalarGridSpec(
+            num_scalar_prefetch=1,
+            grid=(count,),
+            in_specs=[
+                pl.BlockSpec((inner_k, row_count, outer_j, width), lambda n, s: (0, s[0] + n, 0, 0)),
+                pl.BlockSpec(memory_space=pl.ANY),
+            ],
+            out_specs=pl.BlockSpec((1, *shape), lambda n, s: (n, 0, 0)),
+            scratch_shapes=[pltpu.VMEM((width, shape[1]), jnp.float32)],
+        ),
+        compiler_params=pltpu.CompilerParams(vmem_limit_bytes=VMEM),
+        cost_estimate=pl.CostEstimate(
+            flops=0, bytes_accessed=6 * count * shape[0] * shape[1], transcendentals=0
+        ),
+        name="weight_blocks",
+    )(jnp.stack([first, core]).astype(jnp.int32), cycle_integrals, after)
+
+
+def partial_kernel(sources, scalars, *refs):
+    weights, (own, beside, near, far, send_ref, keep_ref) = refs[:-6], refs[-6:]
+    half = len(weights) // 2
+    depth = own.shape[1] * own.shape[2]
+    pieces = [piece[0].reshape(depth, piece.shape[3]) for piece in (own, beside, near, far)]
+    rows = jnp.concatenate(pieces, axis=0)
+    for out, blocks in ((send_ref, weights[:half]), (keep_ref, weights[half:])):
+        matrix = jnp.concatenate([blocks[source][0, scalars[2 + n]] for n, source in enumerate(sources)], axis=1)
+        product = jnp.dot(matrix, rows, preferred_element_type=jnp.float32)
+        out[0] = product.astype(out.dtype).reshape(out.shape[1:])
+
+
+def partial_sums(scalars, sources, weights, amplitudes, index, beside, near, far):
+    _, second, rows, cols = amplitudes.shape
+    lanes = min(LANES, cols)
+    out_rows, depth = weights[0].shape[2:]
+    piece = pl.BlockSpec((1, second, rows, lanes), lambda n, s: (0, 0, 0, n))
+    mine = pl.BlockSpec((1, second, rows, lanes), lambda n, s: (index, 0, 0, n))
+    for_neighbour = [pl.BlockSpec((1, *w.shape[1:]), lambda n, s: (s[0], 0, 0, 0)) for w in weights]
+    for_self = [pl.BlockSpec((1, *w.shape[1:]), lambda n, s: (s[1], 0, 0, 0)) for w in weights]
+    return pl.pallas_call(
+        functools.partial(partial_kernel, sources),
+        out_shape=(
+            jax.ShapeDtypeStruct((1, second, rows, cols), jnp.bfloat16),
+            jax.ShapeDtypeStruct((1, second, rows, cols), jnp.float32),
+        ),
+        grid_spec=pltpu.PrefetchScalarGridSpec(
+            num_scalar_prefetch=1,
+            grid=(cols // lanes,),
+            in_specs=[*for_neighbour, *for_self, mine, mine, piece, piece],
+            out_specs=(piece, piece),
+        ),
+        compiler_params=pltpu.CompilerParams(vmem_limit_bytes=VMEM),
+        cost_estimate=pl.CostEstimate(
+            flops=16 * out_rows * depth * cols,
+            bytes_accessed=14 * second * rows * cols + 16 * out_rows * depth,
+            transcendentals=0,
+        ),
+        name="partial_sums",
+    )(scalars, *weights, *weights, amplitudes, beside, near, far)
+
+
+def finish_kernel(
+    index, e_first, e_second, l_first, l_second, keep, arrived, pair, ladder, e_rows, l_rows, e_cols, l_cols, *rest
+):
+    out_ref, token_ref, coupled = rest[-3:]
+    second = pl.program_id(0)
+    top = ladder.shape[1]
+    cycle = (keep[0, 0] + arrived[0, 0].astype(jnp.float32)).astype(jnp.bfloat16)
+    coupled[...] = cycle.astype(jnp.float32)
+    with_ladder = coupled[pl.ds(0, top), :] + ladder[0]
+    coupled[pl.ds(0, top), :] = with_ladder.astype(jnp.bfloat16).astype(jnp.float32)
+    residual = pair[0, 0].astype(jnp.float32) + coupled[...]
+    denominator = (e_rows[...] - e_first[index] - e_second[second]) + e_cols[...]
+    odd_rows = (l_rows[...] + l_first[index] + l_second[second]) & 1
+    value = jnp.where(odd_rows == l_cols[...] & 1, residual / denominator, 0.0)
+    out_ref[0, 0] = value.astype(jnp.bfloat16)
+    token_ref[...] = jnp.zeros_like(token_ref)
+
+
+def finish(index, occupied, keep, arrived, pair_integrals, ladder, virtual, so_far):
+    count, second, rows, cols = pair_integrals.shape
+    lanes = cols
+    top = ladder.shape[1]
+    one = pl.BlockSpec((1, 1, rows, lanes), lambda j, n, *s: (0, j, 0, n))
+    at_index = pl.BlockSpec((1, 1, rows, lanes), lambda j, n, *s: (index, j, 0, n))
+    by_row = pl.BlockSpec((rows, 1), lambda j, n, *s: (0, 0))
+    by_col = pl.BlockSpec((1, lanes), lambda j, n, *s: (0, n))
+    operands = [*occupied, keep, arrived, pair_integrals, ladder, *virtual]
+    in_specs = [
+        one,
+        one,
+        at_index,
+        pl.BlockSpec((1, top, lanes), lambda j, n, *s: (index * second + j, 0, n)),
+        by_row,
+        by_row,
+        by_col,
+        by_col,
+    ]
+    aliases = {}
+    if so_far is not None:
+        aliases = {len(operands): 0}
+        operands.append(so_far)
+        in_specs.append(pl.BlockSpec(memory_space=pl.ANY))
+    return pl.pallas_call(
+        functools.partial(finish_kernel, index),
+        out_shape=(
+            jax.ShapeDtypeStruct(pair_integrals.shape, jnp.bfloat16),
+            jax.ShapeDtypeStruct((8, 128), jnp.float32),
+        ),
+        grid_spec=pltpu.PrefetchScalarGridSpec(
+            num_scalar_prefetch=4,
+            grid=(second, cols // lanes),
+            in_specs=in_specs,
+            out_specs=(at_index, pl.BlockSpec((8, 128), lambda j, n, *s: (0, 0))),
+            scratch_shapes=[pltpu.VMEM((rows, lanes), jnp.float32)],
+        ),
+        input_output_aliases=aliases,
+        compiler_params=pltpu.CompilerParams(vmem_limit_bytes=VMEM),
+        cost_estimate=pl.CostEstimate(
+            flops=12 * second * rows * cols, bytes_accessed=10 * second * rows * cols, transcendentals=0
+        ),
+        name="finish",
+    )(*operands)
+
+
+def per_device_plane(
+    amplitudes,
+    pair_integrals,
+    cycle_integrals,
+    ladder_integrals,
+    occ_energy,
+    virt_energy,
+    occ_irrep,
+    virt_irrep,
+    slab_i,
+    slab_j,
+):
+    wide_count, narrow_count = lax.axis_size("wide"), lax.axis_size("narrow")
+    wide_index = lax.axis_index("wide")
+    core, x, y = wide_index % 2, wide_index // 2 % 2, wide_index // 4
+    count, second, row_count, virt_count = amplitudes.shape
+    tile_width, _, _, ladder_depth = ladder_integrals.shape
+    tile_rows = count * second * tile_width
+
+    def across(value, bit):
+        return lax.ppermute(value, "wide", [(w, w ^ bit) for w in range(wide_count)])
+
+    by_y = count * 5 // 12
+    first_x, first_y = list(range(count - by_y)), list(range(count - by_y, count))
+    x_queue = [("gather", n) for n in first_x] + [("sum", n) for n in first_y]
+    y_queue = [("gather", n) for n in first_y] + [("sum", n) for n in first_x]
+
+    tile = amplitudes[:, :, :tile_width, :].reshape(tile_rows, virt_count)
+    to_x, to_y, to_both = (lax.ppermute(tile, "wide", [(0, w)]) for w in (XBIT, YBIT, XBIT + YBIT))
+
+    near_blocks = weight_blocks(4 * y, core, 4, cycle_integrals, row_count, tile)
+    same_row = lax.all_gather(near_blocks, "narrow", axis=0)
+    in_row = (x * 2 + core, x * 2 + 1 - core)
+    numbers_x = jnp.stack(
+        [2 * (1 - y) + x, 2 * y + x, *in_row, (1 - x) * 2 + core, (1 - x) * 2 + 1 - core]
+    ).astype(jnp.int32)
+    numbers_y = jnp.stack([2 * y + 1 - x, 2 * y + x, *in_row, core, 1 - core]).astype(jnp.int32)
+
+    label_virt = jnp.repeat(virt_irrep, VBLK)
+    energy_rows = lax.dynamic_slice_in_dim(virt_energy, wide_index * row_count, row_count)
+    label_rows = lax.dynamic_slice_in_dim(label_virt, wide_index * row_count, row_count)
+    occupied = (
+        lookup(slab_i, occ_energy),
+        lookup(slab_j, occ_energy),
+        lookup(slab_i, occ_irrep),
+        lookup(slab_j, occ_irrep),
+    )
+    virtual = (energy_rows[:, None], label_rows[:, None], virt_energy[None, :], label_virt[None, :])
+
+    near, far, sends, kept, tokens = {}, {}, {}, {}, {}
+
+    def sums(index):
+        if index not in sends:
+            if index in first_x:
+                plan = (numbers_x, (0, 0, 0, 0), (same_row,))
+            else:
+                plan = (numbers_y, (0, 0, 1, 1), (same_row, other_row))
+            sends[index], kept[index] = partial_sums(
+                *plan, amplitudes, index, beside, near[index], far[index]
+            )
+        return sends[index]
+
+    def ladder_amplitudes():
+        corner = jnp.where(x == 0, jnp.where(y == 0, tile, to_y), jnp.where(y == 0, to_x, to_both))
+        other = lax.ppermute(corner, "wide", [(w, w + CORE) for w in range(0, wide_count, 2)])
+        every = jnp.where(core == 0, corner, other)
+        every = every.reshape(tile_rows, narrow_count, ladder_depth).transpose(1, 0, 2)
+        return lax.all_to_all(every, "narrow", split_axis=0, concat_axis=0, tiled=True)
+
+    def ladder_chip(every):
+        every = every.reshape(-1, tile_width, ladder_depth)
+        part = jnp.einsum("xcd,acbd->xab", every, ladder_integrals, preferred_element_type=jnp.float32)
+        part = part.reshape(narrow_count, tile_rows, row_count)
+        part = lax.all_to_all(part, "narrow", split_axis=0, concat_axis=0, tiled=True).sum(axis=0)
+        other = lax.ppermute(part, "wide", [(w + CORE, w) for w in range(0, wide_count, 2)])
+        return jnp.concatenate([part, other], axis=1).astype(jnp.bfloat16)
+
+    def packed(value):
+        pieces = virt_count // value.shape[1]
+        flat = jnp.concatenate(jnp.split(value, pieces), axis=1)
+        rows = -(-flat.shape[0] // (16 * second)) * 16
+        return jnp.pad(flat, ((0, rows * second - flat.shape[0]), (0, 0))).reshape(1, second, rows, virt_count)
+
+    def unpacked(value, width):
+        flat = value[:, :, row_count:, :].reshape(-1, virt_count)
+        pieces = virt_count // width
+        return jnp.concatenate(jnp.split(flat[: tile_rows // pieces], pieces, axis=1))
+
+    x_slot, y_slot = 5, 7
+    out, ladder = None, None
+    moved, forwarded, arrived_at, waiting = [], [], [], []
+    for slot in range(count):
+        due = [(XBIT, *x_queue[slot]), (YBIT, *y_queue[slot])]
+        waits, extras, handed_on = [], {}, []
+        if slot == 0:
+            waits += [near_blocks, to_x, to_y, to_both]
+        if slot == 1:
+            waits += [*operands, far_blocks, beside, *occupied, *virtual]
+        if slot >= 2:
+            waits += moved[slot - 2]
+        if slot >= 3:
+            waits += forwarded[slot - 3]
+        if slot == 3:
+            handed_on = [tile_amps]
+        if slot == x_slot:
+            extras = {XBIT: packed(chip_part)}
+        if slot == y_slot:
+            row_part = jnp.concatenate([chip_part, unpacked(moved[x_slot][0], chip_part.shape[1])], axis=1)
+            extras = {YBIT: packed(row_part)}
+        if slot >= by_y and slot + 1 < count:
+            sums(y_queue[slot + 1][1])
+            waits.append(kept[y_queue[slot + 1][1]])
+        if slot >= 9:
+            waits += [tokens[n] for at in arrived_at[: slot - 3] for n in at]
+        cuts = [
+            (amplitudes, index, extras.get(bit)) if kind == "gather" else (sums(index), 0, extras.get(bit))
+            for bit, kind, index in due
+        ]
+        plain = [n for n, (bit, kind, _) in enumerate(due) if kind == "sum" and bit not in extras]
+        sent, passed = launch(
+            [cut for n, cut in enumerate(cuts) if n not in plain], [cuts[n][0] for n in plain] + handed_on, waits
+        )
+        operands = [passed.pop(0) if n in plain else sent.pop(0) for n in range(len(due))]
+        if slot == 0:
+            beside = across(amplitudes, CORE)
+            far_blocks = weight_blocks(4 * (1 - y) + 2 * x, core, 2, cycle_integrals, row_count, operands[0])
+            other_row = lax.all_gather(far_blocks, "narrow", axis=0)
+            tile_amps = ladder_amplitudes()
+        if slot == 3:
+            chip_part = ladder_chip(passed[0])
+        moved.append([])
+        forwarded.append([])
+        arrived_at.append([])
+        for operand, (bit, kind, index) in zip(operands, due):
+            value = across(operand, bit)
+            moved[-1].append(value)
+            if kind == "gather":
+                near[index], far[index] = value, across(value, CORE)
+                forwarded[-1].append(far[index])
+            else:
+                arrived_at[-1].append(index)
+                waiting.append((index, value))
+        if slot == y_slot:
+            parts = [row_part, unpacked(moved[y_slot][1], row_part.shape[1])]
+            ladder = jnp.where(wide_index == 0, jnp.concatenate(parts, axis=1).astype(jnp.float32), 0.0)
+            ladder = ladder.reshape(count * second, tile_width, virt_count)
+        while waiting and slot >= y_slot:
+            index, value = waiting.pop(0)
+            out, tokens[index] = finish(
+                index, occupied, kept[index], value, pair_integrals, ladder, virtual, out
+            )
+    return out
+
+
 def solution(mesh):
+    wide, narrow = mesh.shape["wide"], mesh.shape["narrow"]
+    per_device = per_device_plane if (wide, narrow) == (8, 4) else per_device_any
     return jax.shard_map(
         per_device,
         mesh=mesh,

time: 1110 us -> 397 us (0.36)
  waiting for transfers between devices: 612 us -> 111 us
  local copies, waits for them, and re-layouts: 268 us -> 23.1 us
  Pallas kernels: 0 us -> 186 us
  matrix products: 110 us -> 1.83 us
  other arithmetic: 82.3 us -> 10.3 us
  starting transfers between devices: 12.7 us -> 48.6 us
    all_to_all x2, waiting for transfers between devices: 474 us -> 22.4 us  [the longest x1 22.4 us: ladder_chip(): lax.all_to_all(part, 'narrow', split_axis=0, concat_axis=0, tiled=True)]
    pallas_call x0 -> x38, Pallas kernels: none -> 186 us  [the longest x12 101 us: partial_sums(): pl.pallas_call(functools.partial(partial_kernel, sources), out_shape=(jax...]
    all_gather x2, waiting for transfers between devices: 136 us -> 0.02 us  [the longest x1 0.02 us: per_device_plane(): same_row = lax.all_gather(near_blocks, 'narrow', axis=0)]
    convert_element_type x15 -> x0, local copies, waits for them, and re-layouts: 130 us -> none  [the longest x2 73.1 us: per_device(): residual = pair_integrals.astype(jnp.float32) + coupled.astype(jnp.float32)]
    dot_general x13 -> x1, matrix products: 110 us -> 1.83 us  [ladder_chip(): jnp.einsum('xcd,acbd->xab', every, ladder_integrals, preferred_element_ty...]
    ppermute x0 -> x42, waiting for transfers between devices: none -> 88.8 us  [the longest x37 83.6 us: across(): lax.ppermute(value, 'wide', [(w, w ^ bit) for w in range(wide_count)])]
    convert_element_type x4 -> x0, other arithmetic: 73.1 us -> none  [the longest x1 29.5 us: per_device(): return (allowed * residual / denominator).astype(jnp.bfloat16)]
    unnamed x18 -> x80, local copies, waits for them, and re-layouts: 60.2 us -> 11.3 us
  transfers between devices with their start and end apart: 5 -> 46, of which waited for: 3 -> 14; matrix products, arithmetic and copies ran while one was open for 7% -> 6% of each run, Pallas kernels for 0% -> 46%
where the time goes in v1:
time: 397 us; the launch traced here: 396 us
  Pallas kernels  186 us (47%)
  waiting for transfers between devices  111 us (28%)
  starting transfers between devices  48.6 us (12%)
  local copies, waits for them, and re-layouts  23.1 us (6%)
  between operations  14 us (4%)
  other arithmetic  10.3 us (3%)
    pallas_call x12, Pallas kernels, partial_sums(): pl.pallas_call(functools.partial(partial_kernel, sources), out_shape=(jax...  101 us
    ppermute x37, waiting for transfers between devices, across(): lax.ppermute(value, 'wide', [(w, w ^ bit) for w in range(wide_count)])  83.6 us
    pallas_call x12, Pallas kernels, finish(): pl.pallas_call(functools.partial(finish_kernel, index), out_shape=(jax.Sh...  54.1 us
    ppermute x37, starting transfers between devices, across(): lax.ppermute(value, 'wide', [(w, w ^ bit) for w in range(wide_count)])  26.8 us
    all_to_all x1, waiting for transfers between devices, ladder_chip(): lax.all_to_all(part, 'narrow', split_axis=0, concat_axis=0, tiled=True)  22.4 us
    pallas_call x12, Pallas kernels, launch(): pl.pallas_call(functools.partial(launch_kernel, tuple((extra is not None...  20.3 us
    unnamed x80, local copies, waits for them, and re-layouts  11.3 us
    pallas_call x2, Pallas kernels, weight_blocks(): pl.pallas_call(blocks_kernel, out_shape=jax.ShapeDtypeStruct((count, *sha...  10.7 us
  transfers between devices with their start and end apart: 46, of which 14 were waited for; matrix products, arithmetic and copies ran while one was open for 6% of the time, Pallas kernels for 46%

profile of v1, /device:TPU:0, one launch (start us, length us, event | category | flops | bytes accessed | tf_op | source)
XLA Modules:
  0.0 395.5 jit_solution(15251760506972117411)
XLA Ops:
  9.8 6.4 %weight_blocks.2.refs_2_ = bf16[4,384,384]{2,1,0:T(8,128)(2,1)} custom-call(s32[2]{0:T(128)} %pad_add_fusion.place, bf16[2,1536,2,384]{3,2,1,0:T(2,128)(2,1)} %weights.3, bf16[96,1536]{1,0:T(8,128)(2,1)} %reshape.39.after), custom_call_target="tpu_custom_call" | custom-call | bytes 3538944 | tf_op jit(solution)/shard_map/weight_blocks/pallas_call | solution.py:157
  17.2 5.3 %collective-permute-start.3 = (bf16[96,1536]{1,0:T(8,128)(2,1)S(1)}, bf16[96,1536]{1,0:T(8,128)(2,1)S(1)}, u32[]{:S(2)}, u32[]{:S(2)}) collective-permute-start(bf16[96,1536]{1,0:T(8,128)(2,1)S(1)} %copy-done.13), channel_id=1, source_target_pairs={{0,24},{1,25},{2,26},{3,27}} | collective-permute-start | bytes 884744 | tf_op jit(solution)/shard_map/ppermute | solution.py:312
  42.3 11.1 %collective-permute-done.7.refs_3_.refs_6_ = bf16[1,2,192,1536]{3,2,1,0:T(8,128)(2,1)} collective-permute-done((bf16[1,2,192,1536]{3,2,1,0:T(8,128)(2,1)}, bf16[1,2,192,1536]{3,2,1,0:T(8,128)(2,1)}, u32[]{:S(2)}, u32[]{:S(2)}) %collective-permute-start.7) | collective-permute-done | bytes 1179680 | tf_op jit(solution)/shard_map/ppermute | solution.py:304
  73.4 16.8 %collective-permute-done.4.refs_4_.refs_3_ = bf16[1,2,192,1536]{3,2,1,0:T(8,128)(2,1)} collective-permute-done((bf16[1,2,192,1536]{3,2,1,0:T(8,128)(2,1)}, bf16[1,2,192,1536]{3,2,1,0:T(8,128)(2,1)}, u32[]{:S(2)}, u32[]{:S(2)}) %collective-permute-start.4) | collective-permute-done | bytes 1179680 | tf_op jit(solution)/shard_map/ppermute | solution.py:304
  91.9 4.9 %all-to-all-start = ((bf16[4,96,384]{2,1,0:T(8,128)(2,1)}), bf16[4,96,384]{2,1,0:T(8,128)(2,1)}, u32[]{:S(2)}, u32[]{:S(2)}) async-start(bf16[4,96,384]{2,1,0:T(8,128)(2,1)} %bitcast.68), calls=%async_computation | async-start | bytes 589824 | tf_op jit(solution)/shard_map/all_to_all | solution.py:351
  97.0 18.0 %collective-permute-done.8.refs_2_.refs_4_ = bf16[1,2,192,1536]{3,2,1,0:T(8,128)(2,1)} collective-permute-done((bf16[1,2,192,1536]{3,2,1,0:T(8,128)(2,1)}, bf16[1,2,192,1536]{3,2,1,0:T(8,128)(2,1)}, u32[]{:S(2)}, u32[]{:S(2)}) %collective-permute-start.8) | collective-permute-done | bytes 1179680 | tf_op jit(solution)/shard_map/ppermute | solution.py:304
  126.4 4.9 %all-to-all-start.1 = ((f32[4,96,192]{2,1,0:T(8,128)}), f32[4,96,192]{2,1,0:T(8,128)S(1)}, u32[]{:S(2)}, u32[]{:S(2)}) async-start(f32[4,96,192]{2,1,0:T(8,128)} %reshape.43), calls=%async_computation.1 | async-start | bytes 786432 | tf_op jit(solution)/shard_map/all_to_all | solution.py:357
  132.1 22.4 %all-to-all-done.1 = f32[4,96,192]{2,1,0:T(8,128)S(1)} async-done(((f32[4,96,192]{2,1,0:T(8,128)}), f32[4,96,192]{2,1,0:T(8,128)S(1)}, u32[]{:S(2)}, u32[]{:S(2)}) %all-to-all-start.1) | async-done | bytes 294944 | tf_op jit(solution)/shard_map/all_to_all | solution.py:357
  156.1 8.3 %partial_sums.18 = (bf16[1,2,192,1536]{3,2,1,0:T(8,128)(2,1)}, f32[1,2,192,1536]{3,2,1,0:T(8,128)}) custom-call(s32[6]{0:T(128)} %stack.56.scalars, bf16[4,4,384,384]{3,2,1,0:T(8,128)(2,1)} %bitcast.33, bf16[4,4,384,384]{3,2,1,0:T(8,128)(2,1)} %bitcast.34, bf16[12,2,192,1536]{3,2,1,0:T(8,128)(2,1)} %refs_4_.9, ...), custom_call_target="tpu_custom_call" | custom-call | flops 3623878656 | bytes 10616832 | tf_op jit(solution)/shard_map/partial_sums/pallas_call | solution.py:198
  172.7 8.4 %partial_sums.12 = (bf16[1,2,192,1536]{3,2,1,0:T(8,128)(2,1)}, f32[1,2,192,1536]{3,2,1,0:T(8,128)}) custom-call(s32[6]{0:T(128)} %stack.56.scalars, bf16[4,4,384,384]{3,2,1,0:T(8,128)(2,1)} %bitcast.35, bf16[4,4,384,384]{3,2,1,0:T(8,128)(2,1)} %bitcast.36, bf16[12,2,192,1536]{3,2,1,0:T(8,128)(2,1)} %refs_4_.9, ...), custom_call_target="tpu_custom_call" | custom-call | flops 3623878656 | bytes 10616832 | tf_op jit(solution)/shard_map/partial_sums/pallas_call | solution.py:198
  184.4 8.3 %partial_sums.13 = (bf16[1,2,192,1536]{3,2,1,0:T(8,128)(2,1)}, f32[1,2,192,1536]{3,2,1,0:T(8,128)}) custom-call(s32[6]{0:T(128)} %stack.56.scalars, bf16[4,4,384,384]{3,2,1,0:T(8,128)(2,1)} %bitcast.37, bf16[4,4,384,384]{3,2,1,0:T(8,128)(2,1)} %bitcast.38, bf16[12,2,192,1536]{3,2,1,0:T(8,128)(2,1)} %refs_4_.9, ...), custom_call_target="tpu_custom_call" | custom-call | flops 3623878656 | bytes 10616832 | tf_op jit(solution)/shard_map/partial_sums/pallas_call | solution.py:198
  198.5 8.6 %partial_sums.19 = (bf16[1,2,192,1536]{3,2,1,0:T(8,128)(2,1)}, f32[1,2,192,1536]{3,2,1,0:T(8,128)}) custom-call(s32[6]{0:T(128)} %stack.64.scalars, bf16[4,4,384,384]{3,2,1,0:T(8,128)(2,1)} %bitcast.39, bf16[4,2,384,384]{3,2,1,0:T(8,128)(2,1)} %bitcast.57, bf16[4,4,384,384]{3,2,1,0:T(8,128)(2,1)} %bitcast.40, bf16[4,2,384,384]{3,2,1,0:T(8,128)(2,1)} %bitcast.58, ...), custom_call_target="tpu_custom_call" | custom-call | flops 3623878656 | bytes 10616832 | tf_op jit(solution)/shard_map/partial_sums/pallas_call | solution.py:198
  209.7 8.3 %partial_sums.20 = (bf16[1,2,192,1536]{3,2,1,0:T(8,128)(2,1)}, f32[1,2,192,1536]{3,2,1,0:T(8,128)}) custom-call(s32[6]{0:T(128)} %stack.56.scalars, bf16[4,4,384,384]{3,2,1,0:T(8,128)(2,1)} %bitcast.41, bf16[4,4,384,384]{3,2,1,0:T(8,128)(2,1)} %bitcast.42, bf16[12,2,192,1536]{3,2,1,0:T(8,128)(2,1)} %refs_4_.9, ...), custom_call_target="tpu_custom_call" | custom-call | flops 3623878656 | bytes 10616832 | tf_op jit(solution)/shard_map/partial_sums/pallas_call | solution.py:198
  218.0 5.6 %collective-permute-done.28.refs_3_.refs_4_ = bf16[1,2,208,1536]{3,2,1,0:T(8,128)(2,1)} collective-permute-done((bf16[1,2,208,1536]{3,2,1,0:T(8,128)(2,1)}, bf16[1,2,208,1536]{3,2,1,0:T(8,128)(2,1)}, u32[]{:S(2)}, u32[]{:S(2)}) %collective-permute-start.28) | collective-permute-done | bytes 1277984 | tf_op jit(solution)/shard_map/ppermute | solution.py:304
  231.4 8.6 %partial_sums.16 = (bf16[1,2,192,1536]{3,2,1,0:T(8,128)(2,1)}, f32[1,2,192,1536]{3,2,1,0:T(8,128)}) custom-call(s32[6]{0:T(128)} %stack.64.scalars, bf16[4,4,384,384]{3,2,1,0:T(8,128)(2,1)} %bitcast.44, bf16[4,2,384,384]{3,2,1,0:T(8,128)(2,1)} %bitcast.59, bf16[4,4,384,384]{3,2,1,0:T(8,128)(2,1)} %bitcast.43, bf16[4,2,384,384]{3,2,1,0:T(8,128)(2,1)} %bitcast.60, ...), custom_call_target="tpu_custom_call" | custom-call | flops 3623878656 | bytes 10616832 | tf_op jit(solution)/shard_map/partial_sums/pallas_call | solution.py:198
  240.1 8.8 %partial_sums.23 = (bf16[1,2,192,1536]{3,2,1,0:T(8,128)(2,1)}, f32[1,2,192,1536]{3,2,1,0:T(8,128)}) custom-call(s32[6]{0:T(128)} %stack.64.scalars, bf16[4,4,384,384]{3,2,1,0:T(8,128)(2,1)} %bitcast.45, bf16[4,2,384,384]{3,2,1,0:T(8,128)(2,1)} %bitcast.61, bf16[4,4,384,384]{3,2,1,0:T(8,128)(2,1)} %bitcast.46, bf16[4,2,384,384]{3,2,1,0:T(8,128)(2,1)} %bitcast.62, ...), custom_call_target="tpu_custom_call" | custom-call | flops 3623878656 | bytes 10616832 | tf_op jit(solution)/shard_map/partial_sums/pallas_call | solution.py:198
  250.8 8.3 %partial_sums.17 = (bf16[1,2,192,1536]{3,2,1,0:T(8,128)(2,1)}, f32[1,2,192,1536]{3,2,1,0:T(8,128)}) custom-call(s32[6]{0:T(128)} %stack.56.scalars, bf16[4,4,384,384]{3,2,1,0:T(8,128)(2,1)} %bitcast.47, bf16[4,4,384,384]{3,2,1,0:T(8,128)(2,1)} %bitcast.48, bf16[12,2,192,1536]{3,2,1,0:T(8,128)(2,1)} %refs_4_.9, ...), custom_call_target="tpu_custom_call" | custom-call | flops 3623878656 | bytes 10616832 | tf_op jit(solution)/shard_map/partial_sums/pallas_call | solution.py:198
  260.9 8.2 %partial_sums.21 = (bf16[1,2,192,1536]{3,2,1,0:T(8,128)(2,1)}, f32[1,2,192,1536]{3,2,1,0:T(8,128)}) custom-call(s32[6]{0:T(128)} %stack.56.scalars, bf16[4,4,384,384]{3,2,1,0:T(8,128)(2,1)} %bitcast.49, bf16[4,4,384,384]{3,2,1,0:T(8,128)(2,1)} %bitcast.50, bf16[12,2,192,1536]{3,2,1,0:T(8,128)(2,1)} %refs_4_.9, ...), custom_call_target="tpu_custom_call" | custom-call | flops 3623878656 | bytes 10616832 | tf_op jit(solution)/shard_map/partial_sums/pallas_call | solution.py:198
  269.1 13.0 %collective-permute-done.31.refs_3_.arrived = bf16[1,2,224,1536]{3,2,1,0:T(8,128)(2,1)S(1)} collective-permute-done((bf16[1,2,224,1536]{3,2,1,0:T(8,128)(2,1)}, bf16[1,2,224,1536]{3,2,1,0:T(8,128)(2,1)S(1)}, u32[]{:S(2)}, u32[]{:S(2)}) %collective-permute-start.31) | collective-permute-done | bytes 1376288 | tf_op jit(solution)/shard_map/ppermute | solution.py:304
  289.8 8.6 %partial_sums.22 = (bf16[1,2,192,1536]{3,2,1,0:T(8,128)(2,1)}, f32[1,2,192,1536]{3,2,1,0:T(8,128)}) custom-call(s32[6]{0:T(128)} %stack.64.scalars, bf16[4,4,384,384]{3,2,1,0:T(8,128)(2,1)} %bitcast.51, bf16[4,2,384,384]{3,2,1,0:T(8,128)(2,1)} %bitcast.63, bf16[4,4,384,384]{3,2,1,0:T(8,128)(2,1)} %bitcast.52, bf16[4,2,384,384]{3,2,1,0:T(8,128)(2,1)} %bitcast.64, ...), custom_call_target="tpu_custom_call" | custom-call | flops 3623878656 | bytes 10616832 | tf_op jit(solution)/shard_map/partial_sums/pallas_call | solution.py:198
  298.4 8.6 %partial_sums.15 = (bf16[1,2,192,1536]{3,2,1,0:T(8,128)(2,1)}, f32[1,2,192,1536]{3,2,1,0:T(8,128)}) custom-call(s32[6]{0:T(128)} %stack.64.scalars, bf16[4,4,384,384]{3,2,1,0:T(8,128)(2,1)} %bitcast.53, bf16[4,2,384,384]{3,2,1,0:T(8,128)(2,1)} %bitcast.65, bf16[4,4,384,384]{3,2,1,0:T(8,128)(2,1)} %bitcast.54, bf16[4,2,384,384]{3,2,1,0:T(8,128)(2,1)} %bitcast.66, ...), custom_call_target="tpu_custom_call" | custom-call | flops 3623878656 | bytes 10616832 | tf_op jit(solution)/shard_map/partial_sums/pallas_call | solution.py:198
  307.0 8.5 %partial_sums.14 = (bf16[1,2,192,1536]{3,2,1,0:T(8,128)(2,1)}, f32[1,2,192,1536]{3,2,1,0:T(8,128)}) custom-call(s32[6]{0:T(128)} %stack.56.scalars, bf16[4,4,384,384]{3,2,1,0:T(8,128)(2,1)} %bitcast.55, bf16[4,4,384,384]{3,2,1,0:T(8,128)(2,1)} %bitcast.56, bf16[12,2,192,1536]{3,2,1,0:T(8,128)(2,1)} %refs_4_.9, ...), custom_call_target="tpu_custom_call" | custom-call | flops 3623878656 | bytes 10616832 | tf_op jit(solution)/shard_map/partial_sums/pallas_call | solution.py:198
  364.1 14.4 %collective-permute-done.37.arrived = bf16[1,2,192,1536]{3,2,1,0:T(8,128)(2,1)S(1)} collective-permute-done((bf16[1,2,192,1536]{3,2,1,0:T(8,128)(2,1)}, bf16[1,2,192,1536]{3,2,1,0:T(8,128)(2,1)S(1)}, u32[]{:S(2)}, u32[]{:S(2)}) %collective-permute-start.37) | collective-permute-done | bytes 1179680 | tf_op jit(solution)/shard_map/ppermute | solution.py:304
  384.0 4.6 %finish.23 = (bf16[12,2,192,1536]{3,2,1,0:T(8,128)(2,1)}, f32[8,128]{1,0:T(8,128)}) custom-call(f32[12]{0:T(128)} %select_reduce_fusion.1.refs_6_.e_first, f32[2]{0:T(128)} %select_reduce_fusion.3.refs_7_.e_second, s32[12]{0:T(128)} %select_reduce_fusion.refs_8_.l_first, s32[2]{0:T(128)} %select_reduce_fusion.2.refs_9_.l_second, ...), custom_call_target="tpu_custom_call", output_to_operand_aliasing={{0}: (12, {})} | custom-call | flops 7077888 | bytes 5898240 | tf_op jit(solution)/shard_map/finish/pallas_call | solution.py:262
  (231 shorter events, 152.7 us)
Async XLA Ops:
  6.5 149.5 %all-gather.5.cloned.1.call-start = ((), (), s32[]{:S(2)}) async-start(), calls=%async_computation.2 | async-start | bytes 5898240 | tf_op jit(solution)/shard_map/all_gather | solution.py:315
  6.5 51.8 %collective-permute-start = (bf16[12,2,192,1536]{3,2,1,0:T(8,128)(2,1)}, bf16[12,2,192,1536]{3,2,1,0:T(8,128)(2,1)}, u32[]{:S(2)}, u32[]{:S(2)}) collective-permute-start(bf16[12,2,192,1536]{3,2,1,0:T(8,128)(2,1)} %refs_4_.9), channel_id=1, source_target_pairs={{0,4},{4,0},{8,12},{12,8},{16,20},{20,16},{24,28},{28,24},{1,5},{5... | collective-permute-start | bytes 42467336 | tf_op jit(solution)/shard_map/ppermute | solution.py:304
  16.3 182.2 %all-gather.7.cloned.1.call-start = ((), (), s32[]{:S(2)}) async-start(), calls=%async_computation.3 | async-start | bytes 2949120 | tf_op jit(solution)/shard_map/all_gather | solution.py:410
  70.3 44.8 %collective-permute-start.8 = (bf16[1,2,192,1536]{3,2,1,0:T(8,128)(2,1)}, bf16[1,2,192,1536]{3,2,1,0:T(8,128)(2,1)}, u32[]{:S(2)}, u32[]{:S(2)}) collective-permute-start(bf16[1,2,192,1536]{3,2,1,0:T(8,128)(2,1)} %get-tuple-element.74), channel_id=1, source_target_pairs={{0,8},{4,12},{8,0},{12,4},{16,24},{20,28},{24,16},{28,20},{1,9},{5... | collective-permute-start | bytes 3538952 | tf_op jit(solution)/shard_map/ppermute | solution.py:304
  72.0 43.0 %collective-permute-start.15 = (bf16[1,2,192,1536]{3,2,1,0:T(8,128)(2,1)}, bf16[1,2,192,1536]{3,2,1,0:T(8,128)(2,1)}, u32[]{:S(2)}, u32[]{:S(2)}) collective-permute-start(bf16[1,2,192,1536]{3,2,1,0:T(8,128)(2,1)} %collective-permute-done.6.refs_2_.refs_4_), channel_id=1, source_target_pairs={{0,4},{4,0},{8,12},{12,8},{16,20},{20,16},{24,28},{28,24},{1,5},{5... | collective-permute-start | bytes 3538952 | tf_op jit(solution)/shard_map/ppermute | solution.py:304
  73.1 47.7 %collective-permute-start.9 = (bf16[1,2,192,1536]{3,2,1,0:T(8,128)(2,1)}, bf16[1,2,192,1536]{3,2,1,0:T(8,128)(2,1)S(1)}, u32[]{:S(2)}, u32[]{:S(2)}) collective-permute-start(bf16[1,2,192,1536]{3,2,1,0:T(8,128)(2,1)} %get-tuple-element.75), channel_id=1, source_target_pairs={{0,16},{4,20},{8,24},{12,28},{16,0},{20,4},{24,8},{28,12},{1,17},{... | collective-permute-start | bytes 3538952 | tf_op jit(solution)/shard_map/ppermute | solution.py:304
  90.2 41.1 %collective-permute-start.5 = (bf16[1,2,192,1536]{3,2,1,0:T(8,128)(2,1)}, bf16[1,2,192,1536]{3,2,1,0:T(8,128)(2,1)}, u32[]{:S(2)}, u32[]{:S(2)}) collective-permute-start(bf16[1,2,192,1536]{3,2,1,0:T(8,128)(2,1)} %collective-permute-done.4.refs_4_.refs_3_), channel_id=1, source_target_pairs={{0,4},{4,0},{8,12},{12,8},{16,20},{20,16},{24,28},{28,24},{1,5},{5... | collective-permute-start | bytes 3538952 | tf_op jit(solution)/shard_map/ppermute | solution.py:304
  96.8 57.7 %collective-permute-start.11 = (bf16[1,2,192,1536]{3,2,1,0:T(8,128)(2,1)}, bf16[1,2,192,1536]{3,2,1,0:T(8,128)(2,1)}, u32[]{:S(2)}, u32[]{:S(2)}) collective-permute-start(bf16[1,2,192,1536]{3,2,1,0:T(8,128)(2,1)} %collective-permute-done.10.refs_4_.refs_6_), channel_id=1, source_target_pairs={{0,4},{4,0},{8,12},{12,8},{16,20},{20,16},{24,28},{28,24},{1,5},{5... | collective-permute-start | bytes 3538952 | tf_op jit(solution)/shard_map/ppermute | solution.py:304
  115.1 52.1 %collective-permute-start.21 = (bf16[1,2,192,1536]{3,2,1,0:T(8,128)(2,1)}, bf16[1,2,192,1536]{3,2,1,0:T(8,128)(2,1)}, u32[]{:S(2)}, u32[]{:S(2)}) collective-permute-start(bf16[1,2,192,1536]{3,2,1,0:T(8,128)(2,1)} %collective-permute-done.8.refs_2_.refs_4_), channel_id=1, source_target_pairs={{0,4},{4,0},{8,12},{12,8},{16,20},{20,16},{24,28},{28,24},{1,5},{5... | collective-permute-start | bytes 3538952 | tf_op jit(solution)/shard_map/ppermute | solution.py:304
  117.8 51.6 %collective-permute-start.17 = (bf16[1,2,192,1536]{3,2,1,0:T(8,128)(2,1)}, bf16[1,2,192,1536]{3,2,1,0:T(8,128)(2,1)}, u32[]{:S(2)}, u32[]{:S(2)}) collective-permute-start(bf16[1,2,192,1536]{3,2,1,0:T(8,128)(2,1)} %get-tuple-element.79), channel_id=1, source_target_pairs={{0,8},{4,12},{8,0},{12,4},{16,24},{20,28},{24,16},{28,20},{1,9},{5... | collective-permute-start | bytes 3538952 | tf_op jit(solution)/shard_map/ppermute | solution.py:304
  121.8 50.8 %collective-permute-start.19 = (bf16[1,2,192,1536]{3,2,1,0:T(8,128)(2,1)}, bf16[1,2,192,1536]{3,2,1,0:T(8,128)(2,1)S(1)}, u32[]{:S(2)}, u32[]{:S(2)}) collective-permute-start(bf16[1,2,192,1536]{3,2,1,0:T(8,128)(2,1)} %get-tuple-element.80), channel_id=1, source_target_pairs={{0,16},{4,20},{8,24},{12,28},{16,0},{20,4},{24,8},{28,12},{1,17},{... | collective-permute-start | bytes 3538952 | tf_op jit(solution)/shard_map/ppermute | solution.py:304
  131.3 49.8 %collective-permute-start.25 = (bf16[1,2,192,1536]{3,2,1,0:T(8,128)(2,1)S(1)}, bf16[1,2,192,1536]{3,2,1,0:T(8,128)(2,1)}, u32[]{:S(2)}, u32[]{:S(2)}) collective-permute-start(bf16[1,2,192,1536]{3,2,1,0:T(8,128)(2,1)S(1)} %copy-done.5), channel_id=1, source_target_pairs={{0,4},{4,0},{8,12},{12,8},{16,20},{20,16},{24,28},{28,24},{1,5},{5... | collective-permute-start | bytes 3538952 | tf_op jit(solution)/shard_map/ppermute | solution.py:304
  183.2 40.4 %collective-permute-start.28 = (bf16[1,2,208,1536]{3,2,1,0:T(8,128)(2,1)}, bf16[1,2,208,1536]{3,2,1,0:T(8,128)(2,1)}, u32[]{:S(2)}, u32[]{:S(2)}) collective-permute-start(bf16[1,2,208,1536]{3,2,1,0:T(8,128)(2,1)} %get-tuple-element.92), channel_id=1, source_target_pairs={{0,8},{4,12},{8,0},{12,4},{16,24},{20,28},{24,16},{28,20},{1,9},{5... | collective-permute-start | bytes 3833864 | tf_op jit(solution)/shard_map/ppermute | solution.py:304
  209.3 41.5 %collective-permute-start.22 = (bf16[1,2,192,1536]{3,2,1,0:T(8,128)(2,1)}, bf16[1,2,192,1536]{3,2,1,0:T(8,128)(2,1)}, u32[]{:S(2)}, u32[]{:S(2)}) collective-permute-start(bf16[1,2,192,1536]{3,2,1,0:T(8,128)(2,1)} %get-tuple-element.82), channel_id=1, source_target_pairs={{0,8},{4,12},{8,0},{12,4},{16,24},{20,28},{24,16},{28,20},{1,9},{5... | collective-permute-start | bytes 3538952 | tf_op jit(solution)/shard_map/ppermute | solution.py:304
  229.9 52.2 %collective-permute-start.31 = (bf16[1,2,224,1536]{3,2,1,0:T(8,128)(2,1)}, bf16[1,2,224,1536]{3,2,1,0:T(8,128)(2,1)S(1)}, u32[]{:S(2)}, u32[]{:S(2)}) collective-permute-start(bf16[1,2,224,1536]{3,2,1,0:T(8,128)(2,1)} %get-tuple-element.97), channel_id=1, source_target_pairs={{0,16},{4,20},{8,24},{12,28},{16,0},{20,4},{24,8},{28,12},{1,17},{... | collective-permute-start | bytes 4128776 | tf_op jit(solution)/shard_map/ppermute | solution.py:304
  249.0 39.1 %collective-permute-start.30 = (bf16[1,2,192,1536]{3,2,1,0:T(8,128)(2,1)}, bf16[1,2,192,1536]{3,2,1,0:T(8,128)(2,1)}, u32[]{:S(2)}, u32[]{:S(2)}) collective-permute-start(bf16[1,2,192,1536]{3,2,1,0:T(8,128)(2,1)} %get-tuple-element.96), channel_id=1, source_target_pairs={{0,8},{4,12},{8,0},{12,4},{16,24},{20,28},{24,16},{28,20},{1,9},{5... | collective-permute-start | bytes 3538952 | tf_op jit(solution)/shard_map/ppermute | solution.py:304
  250.8 37.3 %collective-permute-start.23 = (bf16[1,2,192,1536]{3,2,1,0:T(8,128)(2,1)}, bf16[1,2,192,1536]{3,2,1,0:T(8,128)(2,1)}, u32[]{:S(2)}, u32[]{:S(2)}) collective-permute-start(bf16[1,2,192,1536]{3,2,1,0:T(8,128)(2,1)} %collective-permute-done.22.refs_4_.refs_2_), channel_id=1, source_target_pairs={{0,4},{4,0},{8,12},{12,8},{16,20},{20,16},{24,28},{28,24},{1,5},{5... | collective-permute-start | bytes 3538952 | tf_op jit(solution)/shard_map/ppermute | solution.py:304
  260.1 60.0 %collective-permute-start.38 = (bf16[1,2,192,1536]{3,2,1,0:T(8,128)(2,1)}, bf16[1,2,192,1536]{3,2,1,0:T(8,128)(2,1)}, u32[]{:S(2)}, u32[]{:S(2)}) collective-permute-start(bf16[1,2,192,1536]{3,2,1,0:T(8,128)(2,1)} %get-tuple-element.119), channel_id=1, source_target_pairs={{0,8},{4,12},{8,0},{12,4},{16,24},{20,28},{24,16},{28,20},{1,9},{5... | collective-permute-start | bytes 3538952 | tf_op jit(solution)/shard_map/ppermute | solution.py:304
  260.4 59.7 %collective-permute-start.39 = (bf16[1,2,192,1536]{3,2,1,0:T(8,128)(2,1)}, bf16[1,2,192,1536]{3,2,1,0:T(8,128)(2,1)S(1)}, u32[]{:S(2)}, u32[]{:S(2)}) collective-permute-start(bf16[1,2,192,1536]{3,2,1,0:T(8,128)(2,1)} %get-tuple-element.120), channel_id=1, source_target_pairs={{0,16},{4,20},{8,24},{12,28},{16,0},{20,4},{24,8},{28,12},{1,17},{... | collective-permute-start | bytes 3538952 | tf_op jit(solution)/shard_map/ppermute | solution.py:304
  288.1 44.3 %collective-permute-start.33 = (bf16[1,2,192,1536]{3,2,1,0:T(8,128)(2,1)}, bf16[1,2,192,1536]{3,2,1,0:T(8,128)(2,1)S(1)}, u32[]{:S(2)}, u32[]{:S(2)}) collective-permute-start(bf16[1,2,192,1536]{3,2,1,0:T(8,128)(2,1)} %get-tuple-element.101), channel_id=1, source_target_pairs={{0,8},{4,12},{8,0},{12,4},{16,24},{20,28},{24,16},{28,20},{1,9},{5... | collective-permute-start | bytes 3538952 | tf_op jit(solution)/shard_map/ppermute | solution.py:304
  289.8 42.9 %collective-permute-start.34 = (bf16[1,2,192,1536]{3,2,1,0:T(8,128)(2,1)}, bf16[1,2,192,1536]{3,2,1,0:T(8,128)(2,1)S(1)}, u32[]{:S(2)}, u32[]{:S(2)}) collective-permute-start(bf16[1,2,192,1536]{3,2,1,0:T(8,128)(2,1)} %get-tuple-element.102), channel_id=1, source_target_pairs={{0,16},{4,20},{8,24},{12,28},{16,0},{20,4},{24,8},{28,12},{1,17},{... | collective-permute-start | bytes 3538952 | tf_op jit(solution)/shard_map/ppermute | solution.py:304
  321.1 37.5 %collective-permute-start.40 = (bf16[1,2,192,1536]{3,2,1,0:T(8,128)(2,1)}, bf16[1,2,192,1536]{3,2,1,0:T(8,128)(2,1)S(1)}, u32[]{:S(2)}, u32[]{:S(2)}) collective-permute-start(bf16[1,2,192,1536]{3,2,1,0:T(8,128)(2,1)} %get-tuple-element.121), channel_id=1, source_target_pairs={{0,16},{4,20},{8,24},{12,28},{16,0},{20,4},{24,8},{28,12},{1,17},{... | collective-permute-start | bytes 3538952 | tf_op jit(solution)/shard_map/ppermute | solution.py:304
  333.8 44.6 %collective-permute-start.37 = (bf16[1,2,192,1536]{3,2,1,0:T(8,128)(2,1)}, bf16[1,2,192,1536]{3,2,1,0:T(8,128)(2,1)S(1)}, u32[]{:S(2)}, u32[]{:S(2)}) collective-permute-start(bf16[1,2,192,1536]{3,2,1,0:T(8,128)(2,1)} %get-tuple-element.113), channel_id=1, source_target_pairs={{0,8},{4,12},{8,0},{12,4},{16,24},{20,28},{24,16},{28,20},{1,9},{5... | collective-permute-start | bytes 3538952 | tf_op jit(solution)/shard_map/ppermute | solution.py:304
  335.5 48.6 %collective-permute-start.36 = (bf16[1,2,192,1536]{3,2,1,0:T(8,128)(2,1)}, bf16[1,2,192,1536]{3,2,1,0:T(8,128)(2,1)}, u32[]{:S(2)}, u32[]{:S(2)}) collective-permute-start(bf16[1,2,192,1536]{3,2,1,0:T(8,128)(2,1)} %get-tuple-element.111), channel_id=1, source_target_pairs={{0,16},{4,20},{8,24},{12,28},{16,0},{20,4},{24,8},{28,12},{1,17},{... | collective-permute-start | bytes 3538952 | tf_op jit(solution)/shard_map/ppermute | solution.py:304
  (62 other events, 929.2 us)
Sparse Core Ops, SparseCore 0:
  16.4 97.9 all-gather.4
  115.9 57.0 all-gather.6

commit v2 on v0

--- a/solution.py
+++ b/solution.py
@@ -1,9 +1,17 @@
+import functools
+
 import jax
 import jax.numpy as jnp
 from jax import lax
+from jax.experimental import pallas as pl
+from jax.experimental.pallas import tpu as pltpu
 from jax.sharding import PartitionSpec as P
 
 VBLK = 16
+CORE, XBIT, YBIT = 1, 2, 4
+LANES = 512
+VMEM = 60 * 2**20
+COST = pl.CostEstimate(flops=0, bytes_accessed=1, transcendentals=0)
 
 
 def spread(value, axis, source):
@@ -33,7 +41,7 @@
     return lax.map(one_row, amp_rows)
 
 
-def per_device(
+def per_device_any(
     amplitudes,
     pair_integrals,
     cycle_integrals,
@@ -89,7 +97,339 @@
     return (allowed * residual / denominator).astype(jnp.bfloat16)
 
 
+def cut_kernel(copies, passed, *refs):
+    outs = refs[len(refs) - copies - passed :]
+    for source, out in zip(refs[:copies], outs):
+        out[...] = source[...]
+
+
+def cut(amplitudes, pairs, handed_on, waited_for):
+    anywhere = pl.BlockSpec(memory_space=pl.ANY)
+    _, second, rows, cols = amplitudes.shape
+    block = (2, 1, rows, cols)
+    copies = len(pairs)
+    outs = pl.pallas_call(
+        functools.partial(cut_kernel, copies, len(handed_on)),
+        grid=(second if copies else 1,),
+        out_shape=(
+            *(jax.ShapeDtypeStruct((2, second, rows, cols), amplitudes.dtype) for _ in pairs),
+            *(jax.ShapeDtypeStruct(value.shape, value.dtype) for value in handed_on),
+        ),
+        in_specs=[
+            *(pl.BlockSpec(block, lambda j, n=n: (n, j, 0, 0)) for n in pairs),
+            *(anywhere for _ in [*handed_on, *waited_for]),
+        ],
+        out_specs=(
+            *(pl.BlockSpec(block, lambda j: (0, j, 0, 0)) for _ in pairs),
+            *(anywhere for _ in handed_on),
+        ),
+        input_output_aliases={copies + n: copies + n for n in range(len(handed_on))},
+        compiler_params=pltpu.CompilerParams(vmem_limit_bytes=VMEM),
+        cost_estimate=COST,
+        name="cut",
+    )(*[amplitudes] * copies, *handed_on, *waited_for)
+    return outs[:copies], outs[copies:]
+
+
+def blocks_kernel(place, weights, after, out_ref, handed, turned, picked):
+    inner_k, row_count, outer_j, _ = weights.shape
+    depth = inner_k * row_count
+    flat = weights[...].reshape(depth * outer_j, weights.shape[3])
+    mine = pl.ds(pl.multiple_of(place[1] * row_count, row_count), row_count)
+
+    @pl.when(pl.program_id(0) == 0)
+    def _():
+        row = lax.broadcasted_iota(jnp.int32, picked.shape[1:], 0)
+        col = lax.broadcasted_iota(jnp.int32, picked.shape[1:], 1)
+        for j in range(outer_j):
+            picked[j] = (row == outer_j * col + j).astype(picked.dtype)
+
+    for j in range(outer_j):
+        turned[...] = lax.dot_general(flat, picked[j], (((0,), (0,)), ((), ())), preferred_element_type=jnp.float32)
+        out_ref[0, pl.ds(j * row_count, row_count), :] = turned[mine, :].astype(out_ref.dtype)
+
+
+def weight_blocks(first, core, count, cycle_integrals, row_count, after):
+    inner_k, _, outer_j, width = cycle_integrals.shape
+    shape = (outer_j * row_count, inner_k * row_count)
+    return pl.pallas_call(
+        blocks_kernel,
+        out_shape=(
+            jax.ShapeDtypeStruct((count, *shape), cycle_integrals.dtype),
+            jax.ShapeDtypeStruct(after.shape, after.dtype),
+        ),
+        grid_spec=pltpu.PrefetchScalarGridSpec(
+            num_scalar_prefetch=1,
+            grid=(count,),
+            in_specs=[
+                pl.BlockSpec((inner_k, row_count, outer_j, width), lambda n, s: (0, s[0] + n, 0, 0)),
+                pl.BlockSpec(memory_space=pl.ANY),
+            ],
+            out_specs=(pl.BlockSpec((1, *shape), lambda n, s: (n, 0, 0)), pl.BlockSpec(memory_space=pl.ANY)),
+            scratch_shapes=[
+                pltpu.VMEM((width, shape[1]), jnp.float32),
+                pltpu.VMEM((outer_j, shape[1] * outer_j, shape[1]), cycle_integrals.dtype),
+            ],
+        ),
+        input_output_aliases={2: 1},
+        compiler_params=pltpu.CompilerParams(vmem_limit_bytes=VMEM),
+        cost_estimate=COST,
+        name="weight_blocks",
+    )(jnp.stack([first, core]).astype(jnp.int32), cycle_integrals, after)
+
+
+def partial_kernel(sources, outs, scalars, *refs):
+    blocks = len(set(sources))
+    for_neighbour, for_self, refs = refs[:blocks], refs[blocks : 2 * blocks], refs[2 * blocks :]
+    own, beside, near, far = refs[:4]
+    *send, keep = refs[len(refs) - outs :]
+    depth = own.shape[1] * own.shape[2]
+    for unit in range(2):
+        rows = [piece[unit].reshape(depth, piece.shape[3]) for piece in (own, beside, near, far)]
+        rows = jnp.concatenate(rows, axis=0)
+        to_send = send[0].at[unit] if len(send) == 1 else send[unit].at[0]
+        for out, weights in ((to_send, for_neighbour), (keep.at[unit], for_self)):
+            matrix = [weights[source][0, scalars[2 + n]] for n, source in enumerate(sources)]
+            product = jnp.dot(jnp.concatenate(matrix, axis=1), rows, preferred_element_type=jnp.float32)
+            out[...] = product.astype(out.dtype).reshape(out.shape)
+
+
+def partial_sums(scalars, sources, weights, amplitudes, beside, near, far, pair, apart, waited_for):
+    _, second, rows, cols = amplitudes.shape
+    lanes = min(LANES, cols)
+    out_rows, depth = weights[0].shape[2:]
+    mine = pl.BlockSpec((2, second, rows, lanes), lambda n, s: (pair, 0, 0, n))
+    both = pl.BlockSpec((2, second, rows, lanes), lambda n, s: (0, 0, 0, n))
+    one = pl.BlockSpec((1, second, rows, lanes), lambda n, s: (0, 0, 0, n))
+    for_neighbour = [pl.BlockSpec((1, *w.shape[1:]), lambda n, s: (s[0], 0, 0, 0)) for w in weights]
+    for_self = [pl.BlockSpec((1, *w.shape[1:]), lambda n, s: (s[1], 0, 0, 0)) for w in weights]
+    two = (2, second, rows, cols)
+    send_shapes = [(1, *two[1:])] * 2 if apart else [two]
+    outs = pl.pallas_call(
+        functools.partial(partial_kernel, sources, len(send_shapes) + 1),
+        out_shape=(
+            *(jax.ShapeDtypeStruct(shape, jnp.bfloat16) for shape in send_shapes),
+            jax.ShapeDtypeStruct(two, jnp.float32),
+        ),
+        grid_spec=pltpu.PrefetchScalarGridSpec(
+            num_scalar_prefetch=1,
+            grid=(cols // lanes,),
+            in_specs=[
+                *(*for_neighbour, *for_self, mine, mine, both, both),
+                *(pl.BlockSpec(memory_space=pl.ANY) for _ in waited_for),
+            ],
+            out_specs=(*([one, one] if apart else [both]), both),
+        ),
+        compiler_params=pltpu.CompilerParams(vmem_limit_bytes=VMEM),
+        cost_estimate=COST,
+        name="partial_sums",
+    )(scalars, *weights, *weights, amplitudes, beside, near, far, *waited_for)
+    return outs[:-1], outs[-1]
+
+
+def finish_kernel(indices, second_count, slab_i, slab_j, occ_energy, occ_irrep, *refs):
+    units = len(indices)
+    sums, refs = refs[: 2 * units], refs[2 * units :]
+    pair, ladder, e_rows, l_rows, e_cols, l_cols = refs[:6]
+    out_ref, token_ref, coupled = refs[-3:]
+    second = pl.program_id(1)
+    top = ladder.shape[0] // second_count
+    for unit, index in enumerate(indices):
+        keep, arrived = sums[2 * unit : 2 * unit + 2]
+
+        @pl.when(pl.program_id(0) == unit)
+        def _(index=index, keep=keep, arrived=arrived):
+            cycle = (keep[0, 0] + arrived[0, 0].astype(jnp.float32)).astype(jnp.bfloat16)
+            coupled[...] = cycle.astype(jnp.float32)
+            mine = ladder[pl.ds(0, top), :]
+            for j in range(1, ladder.shape[0] // top):
+                mine = jnp.where(second == j, ladder[pl.ds(j * top, top), :], mine)
+            with_ladder = coupled[pl.ds(0, top), :] + mine
+            coupled[pl.ds(0, top), :] = with_ladder.astype(jnp.bfloat16).astype(jnp.float32)
+            residual = pair[0, 0].astype(jnp.float32) + coupled[...]
+            denominator = (e_rows[...] - occ_energy[slab_i[index]] - occ_energy[slab_j[second]]) + e_cols[...]
+            odd_rows = (l_rows[...] + occ_irrep[slab_i[index]] + occ_irrep[slab_j[second]]) & 1
+            value = jnp.where(odd_rows == l_cols[...] & 1, residual / denominator, 0.0)
+            out_ref[0, 0] = value.astype(jnp.bfloat16)
+
+    token_ref[...] = jnp.zeros_like(token_ref)
+
+
+def finish(occupied, units, pair_integrals, ladder, virtual, so_far, after):
+    _, second, rows, cols = pair_integrals.shape
+    top = ladder.shape[0] // pair_integrals.shape[0]
+    indices = tuple(index for index, *_ in units)
+    step = indices[-1] - indices[0]
+    block = (1, 1, rows, cols)
+    at_index = pl.BlockSpec(block, lambda u, j, *s: (indices[0] + u * step, j, 0, 0))
+    by_row = pl.BlockSpec((rows, 1), lambda u, j, *s: (0, 0))
+    by_col = pl.BlockSpec((1, cols), lambda u, j, *s: (0, 0))
+    operands, in_specs = [*occupied], []
+    for unit, (_, *arrays) in enumerate(units):
+        for array, place in arrays:
+            own = lambda u, j, *s, unit=unit, place=place: (
+                place,
+                jnp.where(u == unit, j, jnp.where(u < unit, 0, second - 1)),
+                0,
+                0,
+            )
+            operands.append(array)
+            in_specs.append(pl.BlockSpec(block, own))
+    operands += [pair_integrals, ladder, *virtual]
+    in_specs += [
+        at_index,
+        pl.BlockSpec((top, cols), lambda u, j, *s: (indices[0] + u * step, 0)),
+        by_row,
+        by_row,
+        by_col,
+        by_col,
+    ]
+    operands.append(after)
+    in_specs.append(pl.BlockSpec(memory_space=pl.ANY))
+    aliases = {}
+    if so_far is not None:
+        aliases = {len(operands): 0}
+        operands.append(so_far)
+        in_specs.append(pl.BlockSpec(memory_space=pl.ANY))
+    return pl.pallas_call(
+        functools.partial(finish_kernel, indices, second),
+        out_shape=(
+            jax.ShapeDtypeStruct(pair_integrals.shape, jnp.bfloat16),
+            jax.ShapeDtypeStruct((8, 128), jnp.float32),
+        ),
+        grid_spec=pltpu.PrefetchScalarGridSpec(
+            num_scalar_prefetch=4,
+            grid=(len(units), second),
+            in_specs=in_specs,
+            out_specs=(at_index, pl.BlockSpec((8, 128), lambda u, j, *s: (0, 0))),
+            scratch_shapes=[pltpu.VMEM((rows, cols), jnp.float32)],
+        ),
+        input_output_aliases=aliases,
+        compiler_params=pltpu.CompilerParams(vmem_limit_bytes=VMEM),
+        cost_estimate=COST,
+        name="finish",
+    )(*operands)
+
+
+def per_device_plane(
+    amplitudes,
+    pair_integrals,
+    cycle_integrals,
+    ladder_integrals,
+    occ_energy,
+    virt_energy,
+    occ_irrep,
+    virt_irrep,
+    slab_i,
+    slab_j,
+):
+    wide_count, narrow_count = lax.axis_size("wide"), lax.axis_size("narrow")
+    wide_index = lax.axis_index("wide")
+    core, x, y = wide_index % 2, wide_index // 2 % 2, wide_index // 4
+    count, second, row_count, virt_count = amplitudes.shape
+    tile_width, _, _, ladder_depth = ladder_integrals.shape
+    tile_rows = count * second * tile_width
+
+    def across(value, bit):
+        return lax.ppermute(value, "wide", [(w, w ^ bit) for w in range(wide_count)])
+
+    tile = amplitudes[:, :, :tile_width, :].reshape(tile_rows, virt_count)
+    near_blocks, tile = weight_blocks(4 * y, core, 4, cycle_integrals, row_count, tile)
+    same_row = lax.all_gather(near_blocks, "narrow", axis=0)
+    to_x, to_y, to_both = (lax.ppermute(tile, "wide", [(0, w)]) for w in (XBIT, YBIT, XBIT + YBIT))
+    in_row = (x * 2 + core, x * 2 + 1 - core)
+    numbers_x = jnp.stack(
+        [2 * (1 - y) + x, 2 * y + x, *in_row, (1 - x) * 2 + core, (1 - x) * 2 + 1 - core]
+    ).astype(jnp.int32)
+    numbers_y = jnp.stack([2 * y + 1 - x, 2 * y + x, *in_row, core, 1 - core]).astype(jnp.int32)
+
+    label_virt = jnp.repeat(virt_irrep, VBLK)
+    energy_rows = lax.dynamic_slice_in_dim(virt_energy, wide_index * row_count, row_count)
+    label_rows = lax.dynamic_slice_in_dim(label_virt, wide_index * row_count, row_count)
+    occupied = (slab_i, slab_j, occ_energy, occ_irrep)
+    virtual = (energy_rows[:, None], label_rows[:, None], virt_energy[None, :], label_virt[None, :])
+
+    def ladder_amplitudes(to_x, to_y, to_both):
+        corner = jnp.where(x == 0, jnp.where(y == 0, tile, to_y), jnp.where(y == 0, to_x, to_both))
+        other = lax.ppermute(corner, "wide", [(w, w + CORE) for w in range(0, wide_count, 2)])
+        every = jnp.where(core == 0, corner, other)
+        every = every.reshape(tile_rows, narrow_count, ladder_depth).transpose(1, 0, 2)
+        return lax.all_to_all(every, "narrow", split_axis=0, concat_axis=0, tiled=True)
+
+    def ladder_product(every):
+        every = every.reshape(-1, tile_width, ladder_depth)
+        part = jnp.einsum("xcd,acbd->xab", every, ladder_integrals, preferred_element_type=jnp.float32)
+        return part.reshape(narrow_count, tile_rows, row_count)
+
+    def ladder_chip(part):
+        part = lax.all_to_all(part, "narrow", split_axis=0, concat_axis=0, tiled=True).sum(axis=0)
+        other = lax.ppermute(part, "wide", [(w + CORE, w) for w in range(0, wide_count, 2)])
+        return jnp.concatenate([part, other], axis=1).astype(jnp.bfloat16)
+
+    along_x, along_y = (0, 1, 2, 3), (4, 5)
+    kept, arrived = {}, {}
+
+    def sums(pair, pieces, waited_for):
+        plan = (numbers_x, (0, 0, 0, 0), (same_row,))
+        if pair in along_y:
+            plan = (numbers_y, (0, 0, 1, 1), (same_row, other_row))
+        last = pair in (along_x[-1], along_y[-1])
+        send, kept[pair] = partial_sums(*plan, amplitudes, beside, *pieces, pair, last, waited_for)
+        there = [across(value, YBIT if pair in along_x else XBIT) for value in send]
+        arrived[pair] = [(there[n], 0) if last else (there[0], n) for n in range(2)]
+        return send[0]
+
+    def ends(units, so_far, waited_for):
+        units = [(2 * pair + n, (kept[pair], n), arrived[pair][n]) for pair, n in units]
+        return finish(occupied, units, pair_integrals, ladder, virtual, so_far, waited_for)
+
+    first, _ = cut(amplitudes, (0, 4), [], [near_blocks, to_x, to_y, to_both])
+    beside = across(amplitudes, CORE)
+    near_0, near_4 = across(first[0], XBIT), across(first[1], YBIT)
+    then, to_all = cut(amplitudes, (1, 5), [to_x, to_y, to_both], [*first, beside])
+    near_1, near_5 = across(then[0], XBIT), across(then[1], YBIT)
+    tile_amps = ladder_amplitudes(*to_all)
+    _, (near_0, near_4, tile_amps) = cut(amplitudes, (), [near_0, near_4, tile_amps], [*then])
+    far_0, far_4 = across(near_0, CORE), across(near_4, CORE)
+    far_blocks, ladder_part = weight_blocks(
+        4 * (1 - y) + 2 * x, core, 2, cycle_integrals, row_count, ladder_product(tile_amps)
+    )
+    other_row = lax.all_gather(far_blocks, "narrow", axis=0)
+    chip_part = ladder_chip(ladder_part)
+    third, _ = cut(amplitudes, (2,), [], [*then, far_0, far_4])
+    near_2 = across(third[0], XBIT)
+    after = sums(0, (near_0, far_0), [third[0], chip_part])
+    _, (near_1, near_5, chip_part) = cut(amplitudes, (), [near_1, near_5, chip_part], [after, *virtual])
+    far_1, far_5 = across(near_1, CORE), across(near_5, CORE)
+    from_x = lax.ppermute(chip_part, "wide", [(w + XBIT, w) for w in (0, YBIT)])
+    fourth, _ = cut(amplitudes, (3,), [], [near_1, far_1, far_5])
+    near_3 = across(fourth[0], XBIT)
+    after = sums(1, (near_1, far_1), [fourth[0]])
+    _, (near_2, from_x) = cut(amplitudes, (), [near_2, from_x], [after, arrived[0][0][0]])
+    far_2 = across(near_2, CORE)
+    row_part = jnp.concatenate([chip_part, from_x], axis=1)
+    from_y = lax.ppermute(row_part, "wide", [(YBIT, 0)])
+    after = sums(4, (near_4, far_4), [near_2])
+    after = sums(2, (near_2, far_2), [after])
+    after = sums(5, (near_5, far_5), [after])
+    _, (near_3, from_y) = cut(amplitudes, (), [near_3, from_y], [after, arrived[1][0][0]])
+    far_3 = across(near_3, CORE)
+    ladder = jnp.concatenate([row_part, from_y], axis=1).astype(jnp.float32)
+    ladder = jnp.where(wide_index == 0, ladder, 0.0)
+    after = sums(3, (near_3, far_3), [near_3])
+    out = None
+    for units in ((0, 0), (0, 1)), ((1, 0), (1, 1)), ((2, 0), (2, 1)), ((4, 0), (4, 1)), ((3, 0), (5, 0)), ((3, 1), (5, 1)):
+        out, after = ends(units, out, after)
+    return out
+
+
 def solution(mesh):
+    wide, narrow = mesh.shape["wide"], mesh.shape["narrow"]
+
+    def per_device(amplitudes, *others):
+        fits = (wide, narrow) == (8, 4) and amplitudes.shape[0] == 12
+        return (per_device_plane if fits else per_device_any)(amplitudes, *others)
+
     return jax.shard_map(
         per_device,
         mesh=mesh,

time: 1110 us -> 375 us (0.34)
  waiting for transfers between devices: 612 us -> 133 us
  local copies, waits for them, and re-layouts: 268 us -> 15.2 us
  Pallas kernels: 0 us -> 148 us
  matrix products: 110 us -> 0.87 us
  other arithmetic: 82.3 us -> 4.23 us
  blocking collectives: 0 us -> 26.8 us
  starting transfers between devices: 12.7 us -> 32.6 us
    all_to_all x2 -> x1, waiting for transfers between devices: 474 us -> 0.01 us  [ladder_amplitudes(): lax.all_to_all(every, 'narrow', split_axis=0, concat_axis=0, tiled=True)]
    pallas_call x0 -> x22, Pallas kernels: none -> 148 us  [the longest x6 76.5 us: partial_sums(): pl.pallas_call(functools.partial(partial_kernel, sources, len(send_shapes...]
    all_gather x2, waiting for transfers between devices: 136 us -> 0.01 us  [the longest x1 0.01 us: per_device_plane(): same_row = lax.all_gather(near_blocks, 'narrow', axis=0)]
    ppermute x0 -> x28, waiting for transfers between devices: none -> 133 us  [the longest x21 81.5 us: across(): lax.ppermute(value, 'wide', [(w, w ^ bit) for w in range(wide_count)])]
    convert_element_type x15 -> x0, local copies, waits for them, and re-layouts: 130 us -> none  [the longest x2 73.1 us: per_device(): residual = pair_integrals.astype(jnp.float32) + coupled.astype(jnp.float32)]
    dot_general x13 -> x1, matrix products: 110 us -> 0.87 us  [ladder_product(): jnp.einsum('xcd,acbd->xab', every, ladder_integrals, preferred_element_ty...]
    convert_element_type x4 -> x0, other arithmetic: 73.1 us -> none  [the longest x1 29.5 us: per_device(): return (allowed * residual / denominator).astype(jnp.bfloat16)]
    unnamed x18 -> x34, local copies, waits for them, and re-layouts: 60.2 us -> 5.69 us
  transfers between devices with their start and end apart: 5 -> 31, of which waited for: 3 -> 14; matrix products, arithmetic and copies ran while one was open for 7% -> 4% of each run, Pallas kernels for 0% -> 37%
where the time goes in v2:
time: 375 us; the launch traced here: 374 us
  Pallas kernels  148 us (39%)
  waiting for transfers between devices  133 us (35%)
  starting transfers between devices  32.6 us (9%)
  blocking collectives  26.8 us (7%)
  local copies, waits for them, and re-layouts  15.2 us (4%)
  between operations  13.7 us (4%)
  other arithmetic  4.23 us (1%)
    ppermute x21, waiting for transfers between devices, across(): lax.ppermute(value, 'wide', [(w, w ^ bit) for w in range(wide_count)])  81.5 us
    pallas_call x6, Pallas kernels, partial_sums(): pl.pallas_call(functools.partial(partial_kernel, sources, len(send_shapes...  76.5 us
    pallas_call x6, Pallas kernels, finish(): pl.pallas_call(functools.partial(finish_kernel, indices, second), out_sha...  46 us
    ppermute x1, waiting for transfers between devices, per_device_plane(): from_x = lax.ppermute(chip_part, 'wide', [(w + XBIT, w) for w in (0, YBIT)])  31.3 us
    all_to_all x1, blocking collectives, ladder_chip(): lax.all_to_all(part, 'narrow', split_axis=0, concat_axis=0, tiled=True)  26.8 us
    ppermute x21, starting transfers between devices, across(): lax.ppermute(value, 'wide', [(w, w ^ bit) for w in range(wide_count)])  15.5 us
    pallas_call x8, Pallas kernels, cut(): pl.pallas_call(functools.partial(cut_kernel, copies, len(handed_on)), gri...  13.6 us
    ppermute x1, waiting for transfers between devices, per_device_plane(): from_y = lax.ppermute(row_part, 'wide', [(YBIT, 0)])  12.7 us
  transfers between devices with their start and end apart: 31, of which 14 were waited for; matrix products, arithmetic and copies ran while one was open for 4% of the time, Pallas kernels for 37%

profile of v2, /device:TPU:0, one launch (start us, length us, event | category | flops | bytes accessed | tf_op | source)
XLA Modules:
  0.0 374.1 jit_solution(16982464656918011224)
XLA Ops:
  9.8 6.8 %weight_blocks.2 = (bf16[4,384,384]{2,1,0:T(8,128)(2,1)}, bf16[96,1536]{1,0:T(8,128)(2,1)}) custom-call(s32[2]{0:T(128)} %get-tuple-element.97.place, bf16[2,1536,2,384]{3,2,1,0:T(2,128)(2,1)} %weights.3, bf16[96,1536]{1,0:T(8,128)(2,1)} %reshape.15.after), custom_call_target="tpu_custom_call", output_to_operand_aliasing={{1}: (2, {})} | custom-call | bytes 1 | tf_op jit(solution)/shard_map/weight_blocks/pallas_call | solution.py:155
  16.7 4.4 %collective-permute-start.1 = (bf16[96,1536]{1,0:T(8,128)(2,1)}, bf16[96,1536]{1,0:T(8,128)(2,1)S(1)}, u32[]{:S(2)}, u32[]{:S(2)}) collective-permute-start(bf16[96,1536]{1,0:T(8,128)(2,1)} %get-tuple-element.52), channel_id=1, source_target_pairs={{0,8},{1,9},{2,10},{3,11}} | collective-permute-start | bytes 884744 | tf_op jit(solution)/shard_map/ppermute | solution.py:339
  30.6 4.0 %cut.8 = (bf16[2,2,192,1536]{3,2,1,0:T(8,128)(2,1)}, bf16[2,2,192,1536]{3,2,1,0:T(8,128)(2,1)}) custom-call(bf16[12,2,192,1536]{3,2,1,0:T(8,128)(2,1)} %refs_2_.7, bf16[12,2,192,1536]{3,2,1,0:T(8,128)(2,1)} %refs_2_.7, bf16[4,384,384]{2,1,0:T(8,128)(2,1)} %get-tuple-element.51.refs_2_, bf16[96,1536]{1,0:T(8,128)(2,1)} %copy-done.7, ...), custom_call_target="tpu_custom_call" | custom-call | bytes 1 | tf_op jit(solution)/shard_map/cut/pallas_call | solution.py:111
  38.4 4.0 %cut.9 = (bf16[2,2,192,1536]{3,2,1,0:T(8,128)(2,1)}, bf16[2,2,192,1536]{3,2,1,0:T(8,128)(2,1)}, bf16[96,1536]{1,0:T(8,128)(2,1)}, bf16[96,1536]{1,0:T(8,128)(2,1)}, bf16[96,1536]{1,0:T(8,128)(2,1)}) custom-call(bf16[12,2,192,1536]{3,2,1,0:T(8,128)(2,1)} %refs_2_.7, ...), custom_call_target="tpu_custom_call", output_to_operand_aliasing={{2}: (2, {}), {3}: (3, {}), {4}: (4, {})} | custom-call | bytes 1 | tf_op jit(solution)/shard_map/cut/pallas_call | solution.py:111
  46.7 4.8 %all-to-all-start = ((bf16[4,96,384]{2,1,0:T(8,128)(2,1)}), bf16[4,96,384]{2,1,0:T(8,128)(2,1)S(1)}, u32[]{:S(2)}, u32[]{:S(2)}) async-start(bf16[4,96,384]{2,1,0:T(8,128)(2,1)} %bitcast.28), calls=%async_computation | async-start | bytes 589824 | tf_op jit(solution)/shard_map/all_to_all | solution.py:357
  51.5 27.8 %collective-permute-done.6.refs_0_ = bf16[2,2,192,1536]{3,2,1,0:T(8,128)(2,1)} collective-permute-done((bf16[2,2,192,1536]{3,2,1,0:T(8,128)(2,1)}, bf16[2,2,192,1536]{3,2,1,0:T(8,128)(2,1)}, u32[]{:S(2)}, u32[]{:S(2)}) %collective-permute-start.6) | collective-permute-done | bytes 2359328 | tf_op jit(solution)/shard_map/ppermute | solution.py:334
  87.7 4.8 %weight_blocks.3 = (bf16[2,384,384]{2,1,0:T(8,128)(2,1)}, f32[4,96,192]{2,1,0:T(8,128)}) custom-call(s32[2]{0:T(128)} %get-tuple-element.98.place, bf16[2,1536,2,384]{3,2,1,0:T(2,128)(2,1)} %weights.3, f32[4,96,192]{2,1,0:T(8,128)} %reshape.18.after), custom_call_target="tpu_custom_call", output_to_operand_aliasing={{1}: (2, {})} | custom-call | bytes 1 | tf_op jit(solution)/shard_map/weight_blocks/pallas_call | solution.py:155
  92.4 26.8 %all_to_all.10 = f32[4,96,192]{2,1,0:T(8,128)S(1)} all-to-all(f32[4,96,192]{2,1,0:T(8,128)} %get-tuple-element.61), channel_id=1, replica_groups=mesh['wide'=8,'narrow'=4] {'narrow'}, dimensions={0} | all-to-all | bytes 589824 | tf_op jit(solution)/shard_map/all_to_all | solution.py:365
  127.9 12.7 %partial_sums.6 = (bf16[2,2,192,1536]{3,2,1,0:T(8,128)(2,1)}, f32[2,2,192,1536]{3,2,1,0:T(8,128)}) custom-call(s32[6]{0:T(128)} %stack.56.scalars, bf16[4,4,384,384]{3,2,1,0:T(8,128)(2,1)} %bitcast.29, bf16[4,4,384,384]{3,2,1,0:T(8,128)(2,1)} %bitcast.30, bf16[12,2,192,1536]{3,2,1,0:T(8,128)(2,1)} %refs_2_.7, ...), custom_call_target="tpu_custom_call" | custom-call | bytes 1 | tf_op jit(solution)/shard_map/partial_sums/pallas_call | solution.py:208
  152.6 12.6 %partial_sums.7 = (bf16[2,2,192,1536]{3,2,1,0:T(8,128)(2,1)}, f32[2,2,192,1536]{3,2,1,0:T(8,128)}) custom-call(s32[6]{0:T(128)} %stack.56.scalars, bf16[4,4,384,384]{3,2,1,0:T(8,128)(2,1)} %bitcast.31, bf16[4,4,384,384]{3,2,1,0:T(8,128)(2,1)} %bitcast.32, bf16[12,2,192,1536]{3,2,1,0:T(8,128)(2,1)} %refs_2_.7, ...), custom_call_target="tpu_custom_call" | custom-call | bytes 1 | tf_op jit(solution)/shard_map/partial_sums/pallas_call | solution.py:208
  165.3 31.3 %collective-permute-done.16.refs_1_ = bf16[96,384]{1,0:T(8,128)(2,1)S(1)} collective-permute-done((bf16[96,384]{1,0:T(8,128)(2,1)}, bf16[96,384]{1,0:T(8,128)(2,1)S(1)}, u32[]{:S(2)}, u32[]{:S(2)}) %collective-permute-start.16) | collective-permute-done | bytes 73760 | tf_op jit(solution)/shard_map/ppermute | solution.py:404
  202.2 12.9 %partial_sums.8 = (bf16[2,2,192,1536]{3,2,1,0:T(8,128)(2,1)}, f32[2,2,192,1536]{3,2,1,0:T(8,128)}) custom-call(s32[6]{0:T(128)} %stack.64.scalars, bf16[4,4,384,384]{3,2,1,0:T(8,128)(2,1)} %bitcast.33, bf16[4,2,384,384]{3,2,1,0:T(8,128)(2,1)} %bitcast.41, bf16[4,4,384,384]{3,2,1,0:T(8,128)(2,1)} %bitcast.34, bf16[4,2,384,384]{3,2,1,0:T(8,128)(2,1)} %bitcast.42, ...), custom_call_target="tpu_custom_call" | custom-call | bytes 1 | tf_op jit(solution)/shard_map/partial_sums/pallas_call | solution.py:208
  215.1 12.7 %partial_sums.9 = (bf16[2,2,192,1536]{3,2,1,0:T(8,128)(2,1)}, f32[2,2,192,1536]{3,2,1,0:T(8,128)}) custom-call(s32[6]{0:T(128)} %stack.56.scalars, bf16[4,4,384,384]{3,2,1,0:T(8,128)(2,1)} %bitcast.35, bf16[4,4,384,384]{3,2,1,0:T(8,128)(2,1)} %bitcast.36, bf16[12,2,192,1536]{3,2,1,0:T(8,128)(2,1)} %refs_2_.7, ...), custom_call_target="tpu_custom_call" | custom-call | bytes 1 | tf_op jit(solution)/shard_map/partial_sums/pallas_call | solution.py:208
  227.8 13.0 %partial_sums.10 = (bf16[1,2,192,1536]{3,2,1,0:T(8,128)(2,1)}, bf16[1,2,192,1536]{3,2,1,0:T(8,128)(2,1)}, f32[2,2,192,1536]{3,2,1,0:T(8,128)}) custom-call(s32[6]{0:T(128)} %stack.64.scalars, bf16[4,4,384,384]{3,2,1,0:T(8,128)(2,1)} %bitcast.37, bf16[4,2,384,384]{3,2,1,0:T(8,128)(2,1)} %bitcast.43, bf16[4,4,384,384]{3,2,1,0:T(8,128)(2,1)} %bitcast.38, ...), custom_call_target="tpu_custom_call" | custom-call | bytes 1 | tf_op jit(solution)/shard_map/partial_sums/pallas_call | solution.py:208
  240.8 12.7 %collective-permute-done.18.refs_1_ = bf16[96,768]{1,0:T(8,128)(2,1)S(1)} collective-permute-done((bf16[96,768]{1,0:T(8,128)(2,1)S(1)}, bf16[96,768]{1,0:T(8,128)(2,1)S(1)}, u32[]{:S(2)}, u32[]{:S(2)}) %collective-permute-start.18) | collective-permute-done | bytes 147488 | tf_op jit(solution)/shard_map/ppermute | solution.py:411
  259.8 12.6 %partial_sums.11 = (bf16[1,2,192,1536]{3,2,1,0:T(8,128)(2,1)}, bf16[1,2,192,1536]{3,2,1,0:T(8,128)(2,1)}, f32[2,2,192,1536]{3,2,1,0:T(8,128)}) custom-call(s32[6]{0:T(128)} %stack.56.scalars, bf16[4,4,384,384]{3,2,1,0:T(8,128)(2,1)} %bitcast.39, bf16[4,4,384,384]{3,2,1,0:T(8,128)(2,1)} %bitcast.40, bf16[12,2,192,1536]{3,2,1,0:T(8,128)(2,1)} %refs_2_.7, ...), custom_call_target="tpu_custom_call" | custom-call | bytes 1 | tf_op jit(solution)/shard_map/partial_sums/pallas_call | solution.py:208
  273.6 35.8 %collective-permute-done.27.refs_1_.refs_3_ = bf16[2,2,192,1536]{3,2,1,0:T(8,128)(2,1)} collective-permute-done((bf16[2,2,192,1536]{3,2,1,0:T(8,128)(2,1)}, bf16[2,2,192,1536]{3,2,1,0:T(8,128)(2,1)}, u32[]{:S(2)}, u32[]{:S(2)}) %collective-permute-start.27) | collective-permute-done | bytes 2359328 | tf_op jit(solution)/shard_map/ppermute | solution.py:334
  310.3 7.6 %finish.6 = (bf16[12,2,192,1536]{3,2,1,0:T(8,128)(2,1)}, f32[8,128]{1,0:T(8,128)}) custom-call(s32[12]{0:T(128)} %slab_i.11, s32[2]{0:T(128)} %slab_j.11, f32[300]{0:T(512)} %occ_energy.11, s32[300]{0:T(512)} %occ_irrep.11, f32[2,2,192,1536]{3,2,1,0:T(8,128)} %get-tuple-element.85.refs_0_.refs_2_, ...), custom_call_target="tpu_custom_call" | custom-call | bytes 1 | tf_op jit(solution)/shard_map/finish/pallas_call | solution.py:294
  317.9 7.6 %finish.7 = (bf16[12,2,192,1536]{3,2,1,0:T(8,128)(2,1)}, f32[8,128]{1,0:T(8,128)}) custom-call(s32[12]{0:T(128)} %slab_i.11, s32[2]{0:T(128)} %slab_j.11, f32[300]{0:T(512)} %occ_energy.11, s32[300]{0:T(512)} %occ_irrep.11, f32[2,2,192,1536]{3,2,1,0:T(8,128)} %get-tuple-element.84.refs_0_.refs_2_, ...), custom_call_target="tpu_custom_call", output_to_operand_aliasing={{0}: (15, {})} | custom-call | bytes 1 | tf_op jit(solution)/shard_map/finish/pallas_call | solution.py:294
  325.5 7.6 %finish.8 = (bf16[12,2,192,1536]{3,2,1,0:T(8,128)(2,1)}, f32[8,128]{1,0:T(8,128)}) custom-call(s32[12]{0:T(128)} %slab_i.11, s32[2]{0:T(128)} %slab_j.11, f32[300]{0:T(512)} %occ_energy.11, s32[300]{0:T(512)} %occ_irrep.11, f32[2,2,192,1536]{3,2,1,0:T(8,128)} %get-tuple-element.83.refs_0_.refs_2_, ...), custom_call_target="tpu_custom_call", output_to_operand_aliasing={{0}: (15, {})} | custom-call | bytes 1 | tf_op jit(solution)/shard_map/finish/pallas_call | solution.py:294
  334.6 7.6 %finish.9 = (bf16[12,2,192,1536]{3,2,1,0:T(8,128)(2,1)}, f32[8,128]{1,0:T(8,128)}) custom-call(s32[12]{0:T(128)} %slab_i.11, s32[2]{0:T(128)} %slab_j.11, f32[300]{0:T(512)} %occ_energy.11, s32[300]{0:T(512)} %occ_irrep.11, f32[2,2,192,1536]{3,2,1,0:T(8,128)} %get-tuple-element.82.refs_0_.refs_2_, ...), custom_call_target="tpu_custom_call", output_to_operand_aliasing={{0}: (15, {})} | custom-call | bytes 1 | tf_op jit(solution)/shard_map/finish/pallas_call | solution.py:294
  342.2 7.8 %finish.10 = (bf16[12,2,192,1536]{3,2,1,0:T(8,128)(2,1)}, f32[8,128]{1,0:T(8,128)}) custom-call(s32[12]{0:T(128)} %slab_i.11, s32[2]{0:T(128)} %slab_j.11, f32[300]{0:T(512)} %occ_energy.11, s32[300]{0:T(512)} %occ_irrep.11, f32[2,2,192,1536]{3,2,1,0:T(8,128)} %get-tuple-element.76.refs_0_, ...), custom_call_target="tpu_custom_call", output_to_operand_aliasing={{0}: (15, {})} | custom-call | bytes 1 | tf_op jit(solution)/shard_map/finish/pallas_call | solution.py:294
  350.0 9.5 %collective-permute-done.23.refs_3_ = bf16[1,2,192,1536]{3,2,1,0:T(8,128)(2,1)} collective-permute-done((bf16[1,2,192,1536]{3,2,1,0:T(8,128)(2,1)}, bf16[1,2,192,1536]{3,2,1,0:T(8,128)(2,1)}, u32[]{:S(2)}, u32[]{:S(2)}) %collective-permute-start.23) | collective-permute-done | bytes 1179680 | tf_op jit(solution)/shard_map/ppermute | solution.py:334
  359.5 7.8 %finish.11 = (bf16[12,2,192,1536]{3,2,1,0:T(8,128)(2,1)}, f32[8,128]{1,0:T(8,128)}) custom-call(s32[12]{0:T(128)} %slab_i.11, s32[2]{0:T(128)} %slab_j.11, f32[300]{0:T(512)} %occ_energy.11, s32[300]{0:T(512)} %occ_irrep.11, f32[2,2,192,1536]{3,2,1,0:T(8,128)} %get-tuple-element.76.refs_0_, ...), custom_call_target="tpu_custom_call", output_to_operand_aliasing={{0}: (15, {})} | custom-call | bytes 1 | tf_op jit(solution)/shard_map/finish/pallas_call | solution.py:294
  (121 shorter events, 65.4 us)
Async XLA Ops:
  6.5 121.4 %all-gather.5.cloned.1.call-start = ((), (), s32[]{:S(2)}) async-start(), calls=%async_computation.2 | async-start | bytes 5898240 | tf_op jit(solution)/shard_map/all_gather | solution.py:338
  6.5 31.9 %collective-permute-start = (bf16[12,2,192,1536]{3,2,1,0:T(8,128)(2,1)}, bf16[12,2,192,1536]{3,2,1,0:T(8,128)(2,1)}, u32[]{:S(2)}, u32[]{:S(2)}) collective-permute-start(bf16[12,2,192,1536]{3,2,1,0:T(8,128)(2,1)} %refs_2_.7), channel_id=1, source_target_pairs={{0,4},{4,0},{8,12},{12,8},{16,20},{20,16},{24,28},{28,24},{1,5},{5... | collective-permute-start | bytes 42467336 | tf_op jit(solution)/shard_map/ppermute | solution.py:334
  16.7 8.9 %collective-permute-start.1 = (bf16[96,1536]{1,0:T(8,128)(2,1)}, bf16[96,1536]{1,0:T(8,128)(2,1)S(1)}, u32[]{:S(2)}, u32[]{:S(2)}) collective-permute-start(bf16[96,1536]{1,0:T(8,128)(2,1)} %get-tuple-element.52), channel_id=1, source_target_pairs={{0,8},{1,9},{2,10},{3,11}} | collective-permute-start | bytes 884744 | tf_op jit(solution)/shard_map/ppermute | solution.py:339
  34.6 44.7 %collective-permute-start.6 = (bf16[2,2,192,1536]{3,2,1,0:T(8,128)(2,1)}, bf16[2,2,192,1536]{3,2,1,0:T(8,128)(2,1)}, u32[]{:S(2)}, u32[]{:S(2)}) collective-permute-start(bf16[2,2,192,1536]{3,2,1,0:T(8,128)(2,1)} %get-tuple-element.53.refs_5_), channel_id=1, source_target_pairs={{0,8},{4,12},{8,0},{12,4},{16,24},{20,28},{24,16},{28,20},{1,9},{5... | collective-permute-start | bytes 7077896 | tf_op jit(solution)/shard_map/ppermute | solution.py:334
  34.6 45.7 %collective-permute-start.7 = (bf16[2,2,192,1536]{3,2,1,0:T(8,128)(2,1)}, bf16[2,2,192,1536]{3,2,1,0:T(8,128)(2,1)}, u32[]{:S(2)}, u32[]{:S(2)}) collective-permute-start(bf16[2,2,192,1536]{3,2,1,0:T(8,128)(2,1)} %get-tuple-element.54.refs_6_), channel_id=1, source_target_pairs={{0,16},{4,20},{8,24},{12,28},{16,0},{20,4},{24,8},{28,12},{1,17},{... | collective-permute-start | bytes 7077896 | tf_op jit(solution)/shard_map/ppermute | solution.py:334
  46.7 33.6 %all-to-all-start = ((bf16[4,96,384]{2,1,0:T(8,128)(2,1)}), bf16[4,96,384]{2,1,0:T(8,128)(2,1)S(1)}, u32[]{:S(2)}, u32[]{:S(2)}) async-start(bf16[4,96,384]{2,1,0:T(8,128)(2,1)} %bitcast.28), calls=%async_computation | async-start | bytes 589824 | tf_op jit(solution)/shard_map/all_to_all | solution.py:357
  51.5 150.7 %all-gather.7.cloned.1.call-start = ((), (), s32[]{:S(2)}) async-start(), calls=%async_computation.3 | async-start | bytes 2949120 | tf_op jit(solution)/shard_map/all_gather | solution.py:397
  81.0 44.2 %collective-permute-start.10 = (bf16[2,2,192,1536]{3,2,1,0:T(8,128)(2,1)}, bf16[2,2,192,1536]{3,2,1,0:T(8,128)(2,1)}, u32[]{:S(2)}, u32[]{:S(2)}) collective-permute-start(bf16[2,2,192,1536]{3,2,1,0:T(8,128)(2,1)} %get-tuple-element.62.refs_4_), channel_id=1, source_target_pairs={{0,4},{4,0},{8,12},{12,8},{16,20},{20,16},{24,28},{28,24},{1,5},{5... | collective-permute-start | bytes 7077896 | tf_op jit(solution)/shard_map/ppermute | solution.py:334
  81.0 44.2 %collective-permute-start.11 = (bf16[2,2,192,1536]{3,2,1,0:T(8,128)(2,1)}, bf16[2,2,192,1536]{3,2,1,0:T(8,128)(2,1)}, u32[]{:S(2)}, u32[]{:S(2)}) collective-permute-start(bf16[2,2,192,1536]{3,2,1,0:T(8,128)(2,1)} %get-tuple-element.63.refs_6_), channel_id=1, source_target_pairs={{0,4},{4,0},{8,12},{12,8},{16,20},{20,16},{24,28},{28,24},{1,5},{5... | collective-permute-start | bytes 7077896 | tf_op jit(solution)/shard_map/ppermute | solution.py:334
  81.5 59.1 %collective-permute-start.4 = (bf16[2,2,192,1536]{3,2,1,0:T(8,128)(2,1)}, bf16[2,2,192,1536]{3,2,1,0:T(8,128)(2,1)}, u32[]{:S(2)}, u32[]{:S(2)}) collective-permute-start(bf16[2,2,192,1536]{3,2,1,0:T(8,128)(2,1)} %get-tuple-element.55.refs_3_.refs_1_), channel_id=1, source_target_pairs={{0,8},{4,12},{8,0},{12,4},{16,24},{20,28},{24,16},{28,20},{1,9},{5... | collective-permute-start | bytes 7077896 | tf_op jit(solution)/shard_map/ppermute | solution.py:334
  83.0 57.6 %collective-permute-start.5 = (bf16[2,2,192,1536]{3,2,1,0:T(8,128)(2,1)}, bf16[2,2,192,1536]{3,2,1,0:T(8,128)(2,1)}, u32[]{:S(2)}, u32[]{:S(2)}) collective-permute-start(bf16[2,2,192,1536]{3,2,1,0:T(8,128)(2,1)} %get-tuple-element.56.refs_4_.refs_2_), channel_id=1, source_target_pairs={{0,16},{4,20},{8,24},{12,28},{16,0},{20,4},{24,8},{28,12},{1,17},{... | collective-permute-start | bytes 7077896 | tf_op jit(solution)/shard_map/ppermute | solution.py:334
  141.9 54.6 %collective-permute-start.15 = (bf16[2,2,192,1536]{3,2,1,0:T(8,128)(2,1)}, bf16[2,2,192,1536]{3,2,1,0:T(8,128)(2,1)S(1)}, u32[]{:S(2)}, u32[]{:S(2)}) collective-permute-start(bf16[2,2,192,1536]{3,2,1,0:T(8,128)(2,1)} %cut.11.refs_6_), channel_id=1, source_target_pairs={{0,8},{4,12},{8,0},{12,4},{16,24},{20,28},{24,16},{28,20},{1,9},{5... | collective-permute-start | bytes 7077896 | tf_op jit(solution)/shard_map/ppermute | solution.py:334
  143.0 53.6 %collective-permute-start.17 = (bf16[2,2,192,1536]{3,2,1,0:T(8,128)(2,1)}, bf16[2,2,192,1536]{3,2,1,0:T(8,128)(2,1)}, u32[]{:S(2)}, u32[]{:S(2)}) collective-permute-start(bf16[2,2,192,1536]{3,2,1,0:T(8,128)(2,1)} %get-tuple-element.64.refs_3_), channel_id=1, source_target_pairs={{0,16},{4,20},{8,24},{12,28},{16,0},{20,4},{24,8},{28,12},{1,17},{... | collective-permute-start | bytes 7077896 | tf_op jit(solution)/shard_map/ppermute | solution.py:334
  143.7 52.8 %collective-permute-start.16 = (bf16[96,384]{1,0:T(8,128)(2,1)}, bf16[96,384]{1,0:T(8,128)(2,1)S(1)}, u32[]{:S(2)}, u32[]{:S(2)}) collective-permute-start(bf16[96,384]{1,0:T(8,128)(2,1)} %get-tuple-element.67), channel_id=1, source_target_pairs={{8,0},{24,16},{9,1},{25,17},{10,2},{26,18},{11,3},{27,19}} | collective-permute-start | bytes 221192 | tf_op jit(solution)/shard_map/ppermute | solution.py:404
  198.0 17.1 %collective-permute-start.19 = (bf16[2,2,192,1536]{3,2,1,0:T(8,128)(2,1)}, bf16[2,2,192,1536]{3,2,1,0:T(8,128)(2,1)}, u32[]{:S(2)}, u32[]{:S(2)}) collective-permute-start(bf16[2,2,192,1536]{3,2,1,0:T(8,128)(2,1)} %get-tuple-element.71.refs_8_.refs_4_), channel_id=1, source_target_pairs={{0,4},{4,0},{8,12},{12,8},{16,20},{20,16},{24,28},{28,24},{1,5},{5... | collective-permute-start | bytes 7077896 | tf_op jit(solution)/shard_map/ppermute | solution.py:334
  198.0 55.5 %collective-permute-start.14 = (bf16[2,2,192,1536]{3,2,1,0:T(8,128)(2,1)}, bf16[2,2,192,1536]{3,2,1,0:T(8,128)(2,1)}, u32[]{:S(2)}, u32[]{:S(2)}) collective-permute-start(bf16[2,2,192,1536]{3,2,1,0:T(8,128)(2,1)} %cut.13.refs_6_), channel_id=1, source_target_pairs={{0,8},{4,12},{8,0},{12,4},{16,24},{20,28},{24,16},{28,20},{1,9},{5... | collective-permute-start | bytes 7077896 | tf_op jit(solution)/shard_map/ppermute | solution.py:334
  198.2 55.2 %collective-permute-start.20 = (bf16[2,2,192,1536]{3,2,1,0:T(8,128)(2,1)}, bf16[2,2,192,1536]{3,2,1,0:T(8,128)(2,1)S(1)}, u32[]{:S(2)}, u32[]{:S(2)}) collective-permute-start(bf16[2,2,192,1536]{3,2,1,0:T(8,128)(2,1)} %get-tuple-element.68.refs_2_), channel_id=1, source_target_pairs={{0,16},{4,20},{8,24},{12,28},{16,0},{20,4},{24,8},{28,12},{1,17},{... | collective-permute-start | bytes 7077896 | tf_op jit(solution)/shard_map/ppermute | solution.py:334
  200.0 53.4 %collective-permute-start.18 = (bf16[96,768]{1,0:T(8,128)(2,1)S(1)}, bf16[96,768]{1,0:T(8,128)(2,1)S(1)}, u32[]{:S(2)}, u32[]{:S(2)}) collective-permute-start(bf16[96,768]{1,0:T(8,128)(2,1)S(1)} %pad_maximum_fusion), channel_id=1, source_target_pairs={{16,0},{17,1},{18,2},{19,3}} | collective-permute-start | bytes 442376 | tf_op jit(solution)/shard_map/ppermute | solution.py:411
  254.9 54.4 %collective-permute-start.27 = (bf16[2,2,192,1536]{3,2,1,0:T(8,128)(2,1)}, bf16[2,2,192,1536]{3,2,1,0:T(8,128)(2,1)}, u32[]{:S(2)}, u32[]{:S(2)}) collective-permute-start(bf16[2,2,192,1536]{3,2,1,0:T(8,128)(2,1)} %get-tuple-element.73.refs_8_), channel_id=1, source_target_pairs={{0,16},{4,20},{8,24},{12,28},{16,0},{20,4},{24,8},{28,12},{1,17},{... | collective-permute-start | bytes 7077896 | tf_op jit(solution)/shard_map/ppermute | solution.py:334
  255.0 78.1 %collective-permute-start.26 = (bf16[2,2,192,1536]{3,2,1,0:T(8,128)(2,1)}, bf16[2,2,192,1536]{3,2,1,0:T(8,128)(2,1)S(1)}, u32[]{:S(2)}, u32[]{:S(2)}) collective-permute-start(bf16[2,2,192,1536]{3,2,1,0:T(8,128)(2,1)} %get-tuple-element.72.refs_6_), channel_id=1, source_target_pairs={{0,8},{4,12},{8,0},{12,4},{16,24},{20,28},{24,16},{28,20},{1,9},{5... | collective-permute-start | bytes 7077896 | tf_op jit(solution)/shard_map/ppermute | solution.py:334
  256.2 86.0 %collective-permute-start.25 = (bf16[1,2,192,1536]{3,2,1,0:T(8,128)(2,1)}, bf16[1,2,192,1536]{3,2,1,0:T(8,128)(2,1)}, u32[]{:S(2)}, u32[]{:S(2)}) collective-permute-start(bf16[1,2,192,1536]{3,2,1,0:T(8,128)(2,1)} %get-tuple-element.74.refs_2_), channel_id=1, source_target_pairs={{0,8},{4,12},{8,0},{12,4},{16,24},{20,28},{24,16},{28,20},{1,9},{5... | collective-permute-start | bytes 3538952 | tf_op jit(solution)/shard_map/ppermute | solution.py:334
  272.4 69.8 %collective-permute-start.24 = (bf16[1,2,192,1536]{3,2,1,0:T(8,128)(2,1)}, bf16[1,2,192,1536]{3,2,1,0:T(8,128)(2,1)}, u32[]{:S(2)}, u32[]{:S(2)}) collective-permute-start(bf16[1,2,192,1536]{3,2,1,0:T(8,128)(2,1)} %get-tuple-element.81.refs_10_), channel_id=1, source_target_pairs={{0,16},{4,20},{8,24},{12,28},{16,0},{20,4},{24,8},{28,12},{1,17},{... | collective-permute-start | bytes 3538952 | tf_op jit(solution)/shard_map/ppermute | solution.py:334
  272.4 87.1 %collective-permute-start.23 = (bf16[1,2,192,1536]{3,2,1,0:T(8,128)(2,1)}, bf16[1,2,192,1536]{3,2,1,0:T(8,128)(2,1)}, u32[]{:S(2)}, u32[]{:S(2)}) collective-permute-start(bf16[1,2,192,1536]{3,2,1,0:T(8,128)(2,1)} %get-tuple-element.79), channel_id=1, source_target_pairs={{0,8},{4,12},{8,0},{12,4},{16,24},{20,28},{24,16},{28,20},{1,9},{5... | collective-permute-start | bytes 3538952 | tf_op jit(solution)/shard_map/ppermute | solution.py:334
  309.4 50.1 %collective-permute-start.22 = (bf16[1,2,192,1536]{3,2,1,0:T(8,128)(2,1)}, bf16[1,2,192,1536]{3,2,1,0:T(8,128)(2,1)}, u32[]{:S(2)}, u32[]{:S(2)}) collective-permute-start(bf16[1,2,192,1536]{3,2,1,0:T(8,128)(2,1)} %get-tuple-element.77), channel_id=1, source_target_pairs={{0,16},{4,20},{8,24},{12,28},{16,0},{20,4},{24,8},{28,12},{1,17},{... | collective-permute-start | bytes 3538952 | tf_op jit(solution)/shard_map/ppermute | solution.py:334
  (24 other events, 321.7 us)
Sparse Core Ops, SparseCore 0:
  16.8 106.2 all-gather.4
  143.9 48.1 all-gather.6
